TPU v7x, 32 devices: a whole 2x2x4 slice. The times are simulated.
32 devices in a mesh: det: 2 (over core), ord: 16 (over z, y, x).
Axes of the slice: x: 2, y: 2, z: 4, core: 2. Of those that a mesh axis runs over, the one named last changes fastest.
Arguments:
- wigner: bfloat16 [256, 2, 128, 2048], P('ord', None, None, 'det'), may hold values from -0.125 to 0.125
- alm: bfloat16 [256, 2, 2048], P('ord'), may hold values from -6 to 6
- beam: bfloat16 [64, 2, 2048], replicated, may hold values from -6 to 6
- crossing: int32 [16, 128], P('ord'), may hold values from 0 to 1023, as said below
- offsets: int32 [16, 4096], P('ord'), may hold values from 0 to 124
- fraction: float32 [16, 4096], P('ord'), may hold values from 0 to 1
- taps: float32 [33], replicated, may hold values from -1 to 1
Outputs:
- detector_signal: float32 [64, 65536], P('det', 'ord')
Inputs may be any that keep to these rules, and one draw needn't show every extreme that they name: `crossing`: within one interval's 128 entries at most 16 lie in any one block of 64 consecutive ids; in every draw some block holds exactly 16 entries of every interval.
All inputs are finite; a program needn't handle non-finite values.
Results may differ from a plain program's by a relative error of at most 0.0057.
Values may be sent and summed in bfloat16 or wider, within the bound.
A program may use at most 192 MiB of HBM per device.

v0:
```python
import math

import jax
import jax.numpy as jnp
from jax import lax
from jax.sharding import PartitionSpec as P

TILE = 128


def with_halo(cells, sides, width):
    for axis, dim in sides:
        count = lax.axis_size(axis)
        ends = count - 1
        head = lax.slice_in_dim(cells, 0, width, axis=dim)
        tail = lax.slice_in_dim(cells, cells.shape[dim] - width, cells.shape[dim], axis=dim)
        cells = jnp.concatenate(
            [
                lax.ppermute(tail, axis, [(i, (i + 1) % count) for i in range(ends)]),
                cells,
                lax.ppermute(head, axis, [((i + 1) % count, i) for i in range(ends)]),
            ],
            axis=dim,
        )
    return cells


def lagrange_weights(position):
    shifted = position + 1.0
    minus_one = position - 1.0
    minus_two = position - 2.0
    return (
        -position * minus_one * minus_two / 6.0,
        shifted * minus_one * minus_two / 2.0,
        -shifted * position * minus_two / 2.0,
        shifted * position * minus_one / 6.0,
    )


def stencil_matrix(offset_part, fraction_part, width):
    columns = jnp.arange(width, dtype=jnp.int32)
    distance = columns[:, None] - offset_part[..., None, :]
    factors = lagrange_weights(fraction_part[..., None, :])
    matrix = jnp.zeros(distance.shape, jnp.float32)
    for place in range(4):
        matrix = matrix + jnp.where(distance == place, factors[place], 0.0)
    return matrix


def sky_beam(alm_part, beam_part):
    product = (
        beam_part.astype(jnp.float32)[:, None, :, None, :]
        * alm_part.astype(jnp.float32)[None, :, None, :, :]
    )
    return product.astype(jnp.bfloat16)


def local(wigner, alm, beam, crossing, offsets, fraction, taps):
    det_count = lax.axis_size("det")
    det_index = lax.axis_index("det")
    ord_count = lax.axis_size("ord")
    orders_local = wigner.shape[0]
    half_width = wigner.shape[3]
    det_local = beam.shape[0] // det_count
    alm_half = lax.dynamic_slice_in_dim(alm, det_index * half_width, half_width, 2)
    beam_half = lax.dynamic_slice_in_dim(beam, det_index * half_width, half_width, 2)
    spectra = lax.psum_scatter(
        jnp.einsum(
            "mkrl,jmkcl->jkrcm",
            wigner,
            sky_beam(alm_half, beam_half),
            preferred_element_type=jnp.float32,
        ),
        "det",
        scatter_dimension=0,
        tiled=True,
    )
    items_all = wigner.shape[1] * wigner.shape[2]
    outgoing = spectra.astype(jnp.bfloat16).reshape(det_local, items_all, 2 * orders_local)
    arrived = lax.all_to_all(outgoing, "ord", split_axis=1, concat_axis=2, tiled=True)
    items_local = items_all // ord_count
    spectrum = arrived.reshape(det_local, items_local, ord_count, 2, orders_local).astype(
        jnp.float32
    )
    orders_total = ord_count * orders_local
    longitudes = 2 * orders_total
    block = math.gcd(512, longitudes)
    order_ids = (
        jnp.arange(ord_count, dtype=jnp.int32)[:, None] * orders_local
        + jnp.arange(orders_local, dtype=jnp.int32)[None, :]
    )
    weight_row = (jnp.where(order_ids == 0, 1.0, 2.0) / math.sqrt(longitudes))[:, :, None]
    step_angle = 2.0 * math.pi / longitudes
    base_phase = (
        order_ids[:, :, None] * jnp.arange(block, dtype=jnp.int32)[None, None, :] % longitudes
    )
    base_angle = base_phase.astype(jnp.float32) * step_angle
    base_cos = jnp.cos(base_angle)
    base_sin = jnp.sin(base_angle)
    pieces = []
    for first in range(0, longitudes, block):
        shift_angle = (order_ids * first % longitudes).astype(jnp.float32)[:, :, None] * step_angle
        shift_cos = jnp.cos(shift_angle)
        shift_sin = jnp.sin(shift_angle)
        cos_block = base_cos * shift_cos - base_sin * shift_sin
        sin_block = base_sin * shift_cos + base_cos * shift_sin
        table = jnp.stack([weight_row * cos_block, -weight_row * sin_block], axis=1)
        pieces.append(
            jnp.einsum("jincs,ncsp->ijp", spectrum, table, precision=lax.Precision.HIGHEST)
        )
    cube = jnp.concatenate(pieces, axis=2).astype(jnp.bfloat16)
    tile_width = TILE
    blocks_per_item = longitudes // tile_width
    tiles = cube.reshape(items_local, det_local, blocks_per_item, tile_width).transpose(0, 2, 1, 3)
    tiles = tiles.reshape(items_local * blocks_per_item, det_local, tile_width)
    tiles_local = tiles.shape[0]
    wanted = crossing[0]
    crossings = wanted.shape[0]
    capacity = max(2, 2 * crossings // ord_count)
    holder = wanted // tiles_local
    local_ids = wanted % tiles_local
    order_index = jnp.arange(crossings, dtype=jnp.int32)
    earlier = (holder[:, None] == holder[None, :]) & (order_index[None, :] < order_index[:, None])
    slot_ids = jnp.sum(earlier.astype(jnp.int32), axis=1)
    flat_slot = holder * capacity + slot_ids
    chosen = flat_slot[:, None] == jnp.arange(ord_count * capacity, dtype=jnp.int32)[None, :]
    requests = (jnp.sum(jnp.where(chosen, local_ids[:, None] + 1, 0), axis=0) - 1).reshape(
        ord_count, capacity
    )
    offset_rows = offsets[0].reshape(crossings, -1)
    fraction_rows = fraction[0].reshape(crossings, -1)
    samples_each = offset_rows.shape[1]
    slot_crossing = jnp.sum(jnp.where(chosen, order_index[:, None], 0), axis=0)
    occupied = jnp.any(chosen, axis=0)
    slot_offsets = jnp.where(occupied[:, None], offset_rows[slot_crossing], 0)
    slot_offsets = slot_offsets.reshape(ord_count, capacity, samples_each)
    slot_fractions = jnp.where(occupied[:, None], fraction_rows[slot_crossing], 0.0)
    slot_fractions = slot_fractions.reshape(ord_count, capacity, samples_each)
    asked = lax.all_to_all(requests, "ord", split_axis=0, concat_axis=0, tiled=True)
    asked_offsets = lax.all_to_all(slot_offsets, "ord", split_axis=0, concat_axis=0, tiled=True)
    asked_fractions = lax.all_to_all(slot_fractions, "ord", split_axis=0, concat_axis=0, tiled=True)
    stencil = stencil_matrix(asked_offsets, asked_fractions, tile_width)
    present = asked >= 0
    picked = tiles[jnp.maximum(asked, 0)]
    result = jnp.einsum(
        "rnjo,rnos->rnjs",
        jnp.where(present[..., None, None], picked, jnp.zeros((), jnp.bfloat16)).astype(
            jnp.float32
        ),
        stencil,
        precision=lax.Precision.HIGHEST,
    )
    received = lax.all_to_all(
        result.astype(jnp.bfloat16), "ord", split_axis=0, concat_axis=0, tiled=True
    )
    samples = jnp.transpose(received[holder, slot_ids], (1, 0, 2)).reshape(det_local, -1)
    reach = taps.shape[0] // 2
    extended = with_halo(samples, (("ord", 1),), reach)
    total_time = samples.shape[1]
    padded = jnp.concatenate(
        [extended, jnp.zeros((det_local, 128 - 2 * reach), jnp.bfloat16)], axis=1
    )
    windows = jnp.concatenate(
        [
            padded[:, :total_time].reshape(det_local, -1, 128),
            padded[:, 128 : total_time + 128].reshape(det_local, -1, 128),
        ],
        axis=2,
    )
    lag_index = (
        jnp.arange(256, dtype=jnp.int32)[:, None] - jnp.arange(128, dtype=jnp.int32)[None, :]
    )
    inside = (lag_index >= 0) & (lag_index < taps.shape[0])
    banded = jnp.where(inside, taps[jnp.clip(lag_index, 0, taps.shape[0] - 1)], 0.0)
    smoothed = jnp.einsum(
        "jbu,uo->jbo", windows.astype(jnp.float32), banded, precision=lax.Precision.HIGHEST
    )
    return smoothed.reshape(det_local, total_time)


def solution(mesh):
    return jax.shard_map(
        local,
        mesh=mesh,
        in_specs=(
            P("ord", None, None, "det"),
            P("ord", None, None),
            P(),
            P("ord", None),
            P("ord", None),
            P("ord", None),
            P(),
        ),
        out_specs=P("det", "ord"),
        check_vma=False,
    )
```

profile of v0, /device:TPU:0, one launch (start us, length us, event | category | flops | bytes accessed | tf_op | source)
XLA Modules:
  0.0 159.1 jit_solution(11502221665997296643)
XLA Ops:
  6.5 1.1 dynamic-slice_convert_fusion
  8.8 7.2 %fusion.39 = f32[64,2,128,2,16]{2,0,3,4,1:T(8,128)} fusion(f32[16,2,1024]{2,1,0:T(2,128)S(1)} %dynamic-slice_convert_fusion.1, f32[64,2,1024]{2,0,1:T(8,128)S(1)} %copy.42, bf16[16,2,128,1024]{3,2,1,0:T(8,128)(2,1)} %param.7), kind=kOutput, calls=%fused_computation.37 | convolution fusion | flops 1082130432 | bytes 11141120 | tf_op jit(solution)/shard_map/mkrl,jmkcl->jkrcm/dot_general | solution.py:68
  17.6 8.3 %all-to-all-start = ((s32[16,1,16]{2,1,0:T(1,128)}), s32[16,1,16]{2,1,0:T(1,128)S(1)}, u32[]{:S(2)}, u32[]{:S(2)}) async-start(s32[16,1,16]{2,1,0:T(1,128)} %sub.74), calls=%async_computation | async-start | bytes 16384 | tf_op jit(solution)/shard_map/all_to_all | solution.py:139
  31.1 2.1 %all-to-all-done = s32[16,1,16]{2,1,0:T(1,128)S(1)} async-done(((s32[16,1,16]{2,1,0:T(1,128)}), s32[16,1,16]{2,1,0:T(1,128)S(1)}, u32[]{:S(2)}, u32[]{:S(2)}) %all-to-all-start) | async-done | bytes 1056 | tf_op jit(solution)/shard_map/all_to_all | solution.py:139
  33.2 4.8 %all-to-all-start.3 = ((f32[16,1,512]{2,1,0:T(1,128)}), f32[16,1,512]{2,1,0:T(1,128)S(1)}, u32[]{:S(2)}, u32[]{:S(2)}) async-start(f32[16,1,512]{2,1,0:T(1,128)} %reshape.595), calls=%async_computation.4 | async-start | bytes 65536 | tf_op jit(solution)/shard_map/all_to_all | solution.py:141
  38.8 6.6 %all-to-all-done.3 = f32[16,1,512]{2,1,0:T(1,128)S(1)} async-done(((f32[16,1,512]{2,1,0:T(1,128)}), f32[16,1,512]{2,1,0:T(1,128)S(1)}, u32[]{:S(2)}, u32[]{:S(2)}) %all-to-all-start.3) | async-done | bytes 32800 | tf_op jit(solution)/shard_map/all_to_all | solution.py:141
  45.4 3.4 %all-to-all-start.2 = ((s32[16,1,512]{2,1,0:T(1,128)}), s32[16,1,512]{2,1,0:T(1,128)S(1)}, u32[]{:S(2)}, u32[]{:S(2)}) async-start(s32[16,1,512]{2,1,0:T(1,128)} %reshape.597), calls=%async_computation.3 | async-start | bytes 65536 | tf_op jit(solution)/shard_map/all_to_all | solution.py:140
  49.0 1.3 convert_element_type.53
  51.2 3.0 %copy.45 = bf16[32,256,32]{2,0,1:T(8,128)(2,1)S(1)} copy(bf16[32,256,32]{1,2,0:T(8,128)(2,1)S(1)} %reshape.412) | data formatting | bytes 1048576 | tf_op jit(solution)/shard_map/reshape | solution.py:79
  54.2 2.7 %reshape.599 = bf16[16,2,8192]{2,1,0:T(2,128)(2,1)} reshape(bf16[256,32,32]{2,1,0:T(8,128)(2,1)S(1)} %bitcast.297) | data formatting | bytes 1048576
  56.9 6.9 %all-to-all-start.1 = ((bf16[16,2,8192]{2,1,0:T(2,128)(2,1)}), bf16[16,2,8192]{2,1,0:T(2,128)(2,1)S(1)}, u32[]{:S(2)}, u32[]{:S(2)}) async-start(bf16[16,2,8192]{2,1,0:T(2,128)(2,1)} %reshape.599), calls=%async_computation.2 | async-start | bytes 1048576 | tf_op jit(solution)/shard_map/all_to_all | solution.py:80
  63.8 3.2 %subtract_multiply_fusion = (f32[16,1,16,512]{3,2,0,1:T(8,128)S(1)}, f32[16,1,16,512]{3,2,0,1:T(8,128)}) fusion(s32[16,16]{1,0:T(8,128)S(1)} %iota_add_fusion, f32[16,16]{1,0:T(8,128)S(1)} %get-tuple-element.52, f32[16,16]{1,0:T(8,128)S(1)} %get-tuple-element.53), kind=kLoop, calls=%fused_computation.58 | loop fusion | flops 2621440 | bytes 1051648 | tf_op jit(solution)/shard_map/mul | solution.py:107
  71.3 5.3 %all-to-all-done.1 = bf16[16,2,8192]{2,1,0:T(2,128)(2,1)S(1)} async-done(((bf16[16,2,8192]{2,1,0:T(2,128)(2,1)}), bf16[16,2,8192]{2,1,0:T(2,128)(2,1)S(1)}, u32[]{:S(2)}, u32[]{:S(2)}) %all-to-all-start.1) | async-done | bytes 524320 | tf_op jit(solution)/shard_map/all_to_all | solution.py:80
  77.7 2.6 %copy.47 = bf16[32,16,16,32]{0,3,2,1:T(8,128)(2,1)} copy(bf16[32,16,16,32]{3,0,1,2:T(8,128)(2,1)S(1)} %bitcast.298) | data formatting | bytes 1048576 | tf_op jit(solution)/shard_map/all_to_all | solution.py:80
  80.3 3.6 %fusion.48 = bf16[16,32,512]{2,1,0:T(8,128)(2,1)S(1)} fusion(bf16[32,16,16,2,16]{0,4,3,2,1:T(8,128)(2,1)} %bitcast.301, f32[16,1,16,512]{3,2,0,1:T(8,128)S(1)} %copy-done.1, f32[16,1,16,512]{3,2,0,1:T(8,128)S(1)} %get-tuple-element.17), kind=kOutput, calls=%fused_computation.40 | convolution fusion | flops 1611137024 | bytes 2097152 | tf_op jit(solution)/shard_map/jincs,ncsp->ijp/dot_general | solution.py:109
  84.0 2.2 %gather_fusion = bf16[256,32,128]{2,1,0:T(8,128)(2,1)} fusion(bf16[64,32,128]{2,1,0:T(8,128)(2,1)S(1)} %bitcast.296, s32[1024]{0:T(1024)S(1)} %pad_clamp_fusion.1), kind=kCustom, calls=%fused_computation | custom fusion | bytes 4195328 | tf_op jit(solution)/shard_map/gather | solution.py:144
  86.3 10.6 %fusion.34 = bf16[16,16,32,32]{3,2,1,0:T(8,128)(2,1)S(1)} fusion(f32[16,16,32]{2,1,0:T(8,128)S(1)} %get-tuple-element.15, f32[16,16,32]{2,1,0:T(8,128)S(1)} %copy-done.2, f32[16,16,32]{2,1,0:T(8,128)S(1)} %get-tuple-element.14, f32[16,16,32]{2,1,0:T(8,128)S(1)} %get-tuple-element.13, s32[16,16,32]{2,1,0:T(8,128)S(1)} %copy-done.3, ...), kind=kOutput, calls=%fused_computation.36 | convolution fusion | flops 416546816 | bytes 2785536 | tf_op jit(solution)/shard_map/rnjo,rnos->rnjs/dot_general | solution.py:145
  96.8 2.7 %reshape.601 = bf16[16,2,8192]{2,1,0:T(2,128)(2,1)} reshape(bf16[16,16,32,32]{3,2,1,0:T(8,128)(2,1)S(1)} %fusion.34) | data formatting | bytes 1048576
  99.5 3.9 %all-to-all-start.4 = ((bf16[16,2,8192]{2,1,0:T(2,128)(2,1)}), bf16[16,2,8192]{2,1,0:T(2,128)(2,1)S(1)}, u32[]{:S(2)}, u32[]{:S(2)}) async-start(bf16[16,2,8192]{2,1,0:T(2,128)(2,1)} %reshape.601), calls=%async_computation.5 | async-start | bytes 1048576 | tf_op jit(solution)/shard_map/all_to_all | solution.py:153
  104.2 13.0 %all-to-all-done.4 = bf16[16,2,8192]{2,1,0:T(2,128)(2,1)S(1)} async-done(((bf16[16,2,8192]{2,1,0:T(2,128)(2,1)}), bf16[16,2,8192]{2,1,0:T(2,128)(2,1)S(1)}, u32[]{:S(2)}, u32[]{:S(2)}) %all-to-all-start.4) | async-done | bytes 524320 | tf_op jit(solution)/shard_map/all_to_all | solution.py:153
  120.7 2.5 %collective-permute-start = (bf16[32,16]{1,0:T(8,128)(2,1)S(1)}, bf16[32,16]{1,0:T(8,128)(2,1)S(1)}, u32[]{:S(2)}, u32[]{:S(2)}) collective-permute-start(bf16[32,16]{1,0:T(8,128)(2,1)S(1)} %get-tuple-element.11), channel_id=1, source_target_pairs={{0,1},{1,2},{2,3},{3,4},{4,5},{5,6},{6,7},{7,8},{8,9},{9,10},{10,1... | collective-permute-start | bytes 3080 | tf_op jit(solution)/shard_map/ppermute | solution.py:19
  123.9 1.3 collective-permute-start.1
  125.4 4.0 %collective-permute-done.1 = bf16[32,16]{1,0:T(8,128)(2,1)S(1)} collective-permute-done((bf16[32,16]{1,0:T(8,128)(2,1)S(1)}, bf16[32,16]{1,0:T(8,128)(2,1)S(1)}, u32[]{:S(2)}, u32[]{:S(2)}) %collective-permute-start.1) | collective-permute-done | bytes 1056 | tf_op jit(solution)/shard_map/ppermute | solution.py:21
  129.8 21.4 %fusion.57 = f32[32,32,128]{2,1,0:T(8,128)S(1)} fusion(bf16[32,32,128]{2,1,0:T(8,128)(2,1)S(1)} %bitcast.306, bf16[32,32,128]{2,1,0:T(8,128)(2,1)S(1)} %bitcast.305, f32[]{:T(128)} %bitcast.78, f32[]{:T(128)} %bitcast.79, f32[]{:T(128)} %bitcast.80, f32[]{:T(128)} %bitcast.81, f32[]{:T(128)} %bitcast.82, f32[]{:T(128)} %bitcast.84, f32[]{:T(128)} %bitcast.83, ...), kind=kOutput, calls=%fused_computation.53 | convolution fusion | flops 406126592 | bytes 1048708 | tf_op jit(solution)/shard_map/jbu,uo->jbo/dot_general | solution.py:175
  (84 shorter events, 21.6 us)
Async XLA Ops:
  6.5 42.4 %reduce-scatter.2.cloned.1.call-start = ((), (), s32[]{:S(2)}) async-start(), calls=%async_computation.6 | async-start | bytes 3145728 | tf_op jit(solution)/shard_map/reduce_scatter | solution.py:67
  8.7 7.2 %copy-start.6 = (s32[1,128]{1,0:T(1,128)S(1)}, s32[1,128]{1,0:T(1,128)}, u32[]{:S(2)}) copy-start(s32[1,128]{1,0:T(1,128)} %param.10) | copy-start | bytes 1540
  8.8 17.7 %copy-start.4 = (f32[1,4096]{1,0:T(1,128)S(1)}, f32[1,4096]{1,0:T(1,128)}, u32[]{:S(2)}) copy-start(f32[1,4096]{1,0:T(1,128)} %param.12) | copy-start | bytes 49156
  8.8 19.1 %copy-start.5 = (s32[1,4096]{1,0:T(1,128)S(1)}, s32[1,4096]{1,0:T(1,128)}, u32[]{:S(2)}) copy-start(s32[1,4096]{1,0:T(1,128)} %param.11) | copy-start | bytes 49156
  16.2 0.6 copy-start.8
  17.6 15.6 %all-to-all-start = ((s32[16,1,16]{2,1,0:T(1,128)}), s32[16,1,16]{2,1,0:T(1,128)S(1)}, u32[]{:S(2)}, u32[]{:S(2)}) async-start(s32[16,1,16]{2,1,0:T(1,128)} %sub.74), calls=%async_computation | async-start | bytes 16384 | tf_op jit(solution)/shard_map/all_to_all | solution.py:139
  33.2 12.3 %all-to-all-start.3 = ((f32[16,1,512]{2,1,0:T(1,128)}), f32[16,1,512]{2,1,0:T(1,128)S(1)}, u32[]{:S(2)}, u32[]{:S(2)}) async-start(f32[16,1,512]{2,1,0:T(1,128)} %reshape.595), calls=%async_computation.4 | async-start | bytes 65536 | tf_op jit(solution)/shard_map/all_to_all | solution.py:141
  45.4 11.4 %all-to-all-start.2 = ((s32[16,1,512]{2,1,0:T(1,128)}), s32[16,1,512]{2,1,0:T(1,128)S(1)}, u32[]{:S(2)}, u32[]{:S(2)}) async-start(s32[16,1,512]{2,1,0:T(1,128)} %reshape.597), calls=%async_computation.3 | async-start | bytes 65536 | tf_op jit(solution)/shard_map/all_to_all | solution.py:140
  56.9 19.7 %all-to-all-start.1 = ((bf16[16,2,8192]{2,1,0:T(2,128)(2,1)}), bf16[16,2,8192]{2,1,0:T(2,128)(2,1)S(1)}, u32[]{:S(2)}, u32[]{:S(2)}) async-start(bf16[16,2,8192]{2,1,0:T(2,128)(2,1)} %reshape.599), calls=%async_computation.2 | async-start | bytes 1048576 | tf_op jit(solution)/shard_map/all_to_all | solution.py:80
  77.6 2.6 %copy-start.1 = (f32[16,1,16,512]{3,2,0,1:T(8,128)S(1)}, f32[16,1,16,512]{3,2,0,1:T(8,128)}, u32[]{:S(2)}) copy-start(f32[16,1,16,512]{3,2,0,1:T(8,128)} %get-tuple-element.18) | copy-start | bytes 1572868
  83.9 2.4 %copy-start.2 = (f32[16,16,32]{2,1,0:T(8,128)S(1)}, f32[16,16,32]{2,1,0:T(8,128)}, u32[]{:S(2)}) copy-start(f32[16,16,32]{2,1,0:T(8,128)} %get-tuple-element.16) | copy-start | bytes 98308
  83.9 2.4 %copy-start.3 = (s32[16,16,32]{2,1,0:T(8,128)S(1)}, s32[16,16,32]{2,1,0:T(8,128)}, u32[]{:S(2)}) copy-start(s32[16,16,32]{2,1,0:T(8,128)} %reshape.598) | copy-start | bytes 98308
  86.3 17.2 %copy-start = (f32[33]{0:T(128)S(1)}, f32[33]{0:T(128)}, u32[]{:S(2)}) copy-start(f32[33]{0:T(128)} %param.13) | copy-start | bytes 400
  86.3 17.9 %copy-start.7 = (s32[1,128]{1,0:T(1,128)S(1)}, s32[1,128]{1,0:T(1,128)}, u32[]{:S(2)}) copy-start(s32[1,128]{1,0:T(1,128)} %param.10) | copy-start | bytes 1540
  86.3 17.9 %copy-start.9 = (s32[128]{0:T(128)S(1)}, s32[128]{0:T(128)}, u32[]{:S(2)}) copy-start(s32[128]{0:T(128)} %copy-done.8) | copy-start | bytes 1540
  99.5 17.6 %all-to-all-start.4 = ((bf16[16,2,8192]{2,1,0:T(2,128)(2,1)}), bf16[16,2,8192]{2,1,0:T(2,128)(2,1)S(1)}, u32[]{:S(2)}, u32[]{:S(2)}) async-start(bf16[16,2,8192]{2,1,0:T(2,128)(2,1)} %reshape.601), calls=%async_computation.5 | async-start | bytes 1048576 | tf_op jit(solution)/shard_map/all_to_all | solution.py:153
  120.7 4.5 %collective-permute-start = (bf16[32,16]{1,0:T(8,128)(2,1)S(1)}, bf16[32,16]{1,0:T(8,128)(2,1)S(1)}, u32[]{:S(2)}, u32[]{:S(2)}) collective-permute-start(bf16[32,16]{1,0:T(8,128)(2,1)S(1)} %get-tuple-element.11), channel_id=1, source_target_pairs={{0,1},{1,2},{2,3},{3,4},{4,5},{5,6},{6,7},{7,8},{8,9},{9,10},{10,1... | collective-permute-start | bytes 3080 | tf_op jit(solution)/shard_map/ppermute | solution.py:19
  123.9 5.5 %collective-permute-start.1 = (bf16[32,16]{1,0:T(8,128)(2,1)S(1)}, bf16[32,16]{1,0:T(8,128)(2,1)S(1)}, u32[]{:S(2)}, u32[]{:S(2)}) collective-permute-start(bf16[32,16]{1,0:T(8,128)(2,1)S(1)} %get-tuple-element.12), channel_id=1, source_target_pairs={{1,0},{2,1},{3,2},{4,3},{5,4},{6,5},{7,6},{8,7},{9,8},{10,9},{11,1... | collective-permute-start | bytes 3080 | tf_op jit(solution)/shard_map/ppermute | solution.py:21
Sparse Core Ops, SparseCore 0:
  16.1 12.2 reduce-scatter.1
where the time goes:
time: 161 us; the launch traced here: 159 us
  matrix products  42.7 us (27%)
  starting transfers between devices  31.1 us (19%)
  waiting for transfers between devices  31 us (19%)
  local copies, waits for them, and re-layouts  29.3 us (18%)
  between operations  13.8 us (9%)
  other arithmetic  11.2 us (7%)
    dot_general x1, matrix products, local(): jnp.einsum('jbu,uo->jbo', windows.astype(jnp.float32), banded, precision=...  21.4 us
    all_to_all x1, waiting for transfers between devices, local(): lax.all_to_all(result.astype(jnp.bfloat16), 'ord', split_axis=0, concat_a...  13 us
    unnamed x34, local copies, waits for them, and re-layouts  12.6 us
    dot_general x1, matrix products, local(): jnp.einsum('rnjo,rnos->rnjs', jnp.where(present[..., None, None], picked,...  10.6 us
    all_to_all x1, starting transfers between devices, local(): lax.all_to_all(requests, 'ord', split_axis=0, concat_axis=0, tiled=True)  8.32 us
    dot_general x1, matrix products, local(): jnp.einsum('mkrl,jmkcl->jkrcm', wigner, sky_beam(alm_half, beam_half), pr...  7.18 us
    all_to_all x1, starting transfers between devices, local(): lax.all_to_all(outgoing, 'ord', split_axis=1, concat_axis=2, tiled=True)  6.89 us
    all_to_all x1, waiting for transfers between devices, local(): lax.all_to_all(slot_fractions, 'ord', split_axis=0, concat_axis=0, tiled=...  6.61 us
  transfers between devices with their start and end apart: 8, of which 5 were waited for; matrix products, arithmetic and copies ran while one was open for 15% of the time, Pallas kernels for 0%

commit v1 on v0

--- a/solution.py
+++ b/solution.py
@@ -1,11 +1,427 @@
+import functools
 import math
 
 import jax
 import jax.numpy as jnp
+import numpy as np
 from jax import lax
+from jax.experimental import pallas as pl
+from jax.experimental.pallas import tpu as pltpu
 from jax.sharding import PartitionSpec as P
 
 TILE = 128
+CHUNKS = 4
+INFO_ROWS = 40
+MESH = pl.DeviceIdType.MESH
+
+
+def split_parts(values):
+    high = values.astype(jnp.bfloat16)
+    return high, (values - high.astype(jnp.float32)).astype(jnp.bfloat16)
+
+
+def fourier_tables(orders_total, per):
+    longitudes = 2 * orders_total
+    order = np.arange(orders_total, dtype=np.int64)
+    phase = (order[:, None] * np.arange(longitudes)[None, :]) % longitudes
+    angle = phase * (2.0 * math.pi / longitudes)
+    weight = np.where(order == 0, 1.0, 2.0)[:, None] / math.sqrt(longitudes)
+    parts = np.stack([weight * np.cos(angle), -weight * np.sin(angle)], axis=1)
+    parts = parts.reshape(orders_total, 2, longitudes // TILE, TILE)
+    table = np.zeros((orders_total, per, 2, longitudes // TILE, per, TILE), np.float32)
+    for det in range(per):
+        table[:, det, :, :, det, :] = parts
+    table = table.reshape(orders_total * per * 2, longitudes * per)
+    high = table.astype(jnp.bfloat16)
+    low = (table - high.astype(np.float32)).astype(jnp.bfloat16)
+    return np.stack([high, low])
+
+
+def kernel(
+    count, per, intervals, tiles_per_item,
+    wigner_hbm, beam_ref, alm_ref, table_hbm, info_ref, taps_ref,
+    out_ref,
+    wigner, table, partial_own, partial_out, partial_in, spectra_out, spectra_in,
+    info, picks, shifts, weights, band, cube, series, signal_out,
+    wigner_sem, table_sem, info_send, info_recv, share_send, share_recv,
+    pair_send, pair_recv, spec_send, spec_recv, out_send, out_recv,
+):
+    det = lax.axis_index("det")
+    me = lax.axis_index("ord")
+    partner = 1 - det
+    orders = wigner.shape[0]
+    chunk_orders = orders // CHUNKS
+    blocks = shifts.shape[2]
+    groups = tiles_per_item
+
+    def wigner_copy(chunk):
+        part = pl.ds(chunk * chunk_orders, chunk_orders)
+        return pltpu.make_async_copy(wigner_hbm.at[part], wigner.at[part], wigner_sem.at[chunk])
+
+    for chunk in range(CHUNKS):
+        wigner_copy(chunk).start()
+    table_copy = pltpu.make_async_copy(table_hbm, table, table_sem)
+    table_copy.start()
+
+    barrier = pltpu.get_barrier_semaphore()
+
+    def greet(step, carry):
+        peer = lax.rem(me + step, count)
+        pl.semaphore_signal(barrier, inc=1, device_id=(det, peer), device_id_type=MESH)
+        return carry
+
+    lax.fori_loop(1, count, greet, 0)
+    pl.semaphore_signal(barrier, inc=1, device_id=(partner, me), device_id_type=MESH)
+    pl.semaphore_wait(barrier, count)
+
+    info[det, me] = info_ref[...]
+
+    def info_copy(target, source):
+        return pltpu.make_async_remote_copy(
+            src_ref=info_ref,
+            dst_ref=info.at[det, source],
+            send_sem=info_send.at[target],
+            recv_sem=info_recv.at[source],
+            device_id=(det, target),
+            device_id_type=MESH,
+        )
+
+    def info_start(step, carry):
+        info_copy(lax.rem(me + step, count), me).start()
+        return carry
+
+    lax.fori_loop(1, count, info_start, 0)
+
+    rows = per * 2
+    own_rows = count * rows
+
+    def product(order, beam_order):
+        alm_rows = alm_ref[order]
+        beam_rows = beam_ref[beam_order]
+        depth = beam_rows.shape[1]
+        sky = beam_rows.reshape(-1, alm_rows.shape[0], depth) * alm_rows[None]
+        return lax.dot_general(
+            sky.reshape(-1, depth),
+            wigner[order, beam_order],
+            (((1,), (1,)), ((), ())),
+            preferred_element_type=jnp.float32,
+        )
+
+    def multiply(chunk):
+        wigner_copy(chunk).wait()
+
+        def pair(step, carry):
+            first = chunk * chunk_orders + 2 * step
+            place = pl.ds(pl.multiple_of(step * 2 * rows, 2 * rows), 2 * rows)
+            for beam_order in range(wigner.shape[1]):
+                lanes = pl.ds(beam_order * wigner.shape[2], wigner.shape[2])
+                one = product(first, beam_order)
+                two = product(first + 1, beam_order)
+                for target, low in ((partial_own, 0), (partial_out, own_rows)):
+                    target[chunk, :, place, lanes] = jnp.concatenate(
+                        [
+                            one[low : low + own_rows].reshape(count, rows, -1),
+                            two[low : low + own_rows].reshape(count, rows, -1),
+                        ],
+                        axis=1,
+                    )
+            return carry
+
+        lax.fori_loop(0, chunk_orders // 2, pair, 0)
+
+    def pair_copy(chunk):
+        return pltpu.make_async_remote_copy(
+            src_ref=partial_out.at[chunk],
+            dst_ref=partial_in.at[chunk],
+            send_sem=pair_send.at[chunk],
+            recv_sem=pair_recv.at[chunk],
+            device_id=(partner, me),
+            device_id_type=MESH,
+        )
+
+    def spec_copy(chunk, target, source):
+        return pltpu.make_async_remote_copy(
+            src_ref=spectra_out.at[chunk, target],
+            dst_ref=spectra_in.at[source, chunk],
+            send_sem=spec_send.at[chunk, target],
+            recv_sem=spec_recv.at[chunk, source],
+            device_id=(det, target),
+            device_id_type=MESH,
+        )
+
+    def spread(chunk):
+        pair_copy(chunk).wait_recv()
+        total = (partial_own[chunk] + partial_in[chunk]).astype(jnp.bfloat16)
+        spectra_out[chunk] = total
+
+        def start(step, carry):
+            spec_copy(chunk, lax.rem(me + step, count), me).start()
+            return carry
+
+        lax.fori_loop(1, count, start, 0)
+        spectra_in[me, chunk] = spectra_out[chunk, me]
+
+    for chunk in range(CHUNKS):
+        multiply(chunk)
+        pair_copy(chunk).start()
+        if chunk > 0:
+            spread(chunk - 1)
+    spread(CHUNKS - 1)
+
+    def info_wait(step, carry):
+        source = lax.rem(me + count - step, count)
+        info_copy(source, source).wait_recv()
+        return carry
+
+    lax.fori_loop(1, count, info_wait, 0)
+    share_copy = pltpu.make_async_remote_copy(
+        src_ref=info.at[det],
+        dst_ref=info.at[det],
+        send_sem=share_send,
+        recv_sem=share_recv,
+        device_id=(partner, me),
+        device_id_type=MESH,
+    )
+    share_copy.start()
+
+    shape = (3 * TILE, TILE)
+    lag = (
+        lax.broadcasted_iota(jnp.int32, shape, 0) - lax.broadcasted_iota(jnp.int32, shape, 1)
+    )
+    reach = taps_ref.shape[0] // 2
+
+    def add_tap(place, total):
+        return jnp.where(lag == place + (TILE - reach), taps_ref[place], total)
+
+    band_values = lax.fori_loop(0, taps_ref.shape[0], add_tap, jnp.zeros(shape, jnp.float32))
+    band_high, band_low = split_parts(band_values)
+    band[0] = band_high
+    band[1] = band_low
+
+    pltpu.make_async_remote_copy(
+        src_ref=info.at[partner],
+        dst_ref=info.at[partner],
+        send_sem=share_send,
+        recv_sem=share_recv,
+        device_id=(partner, me),
+        device_id_type=MESH,
+    ).wait_recv()
+
+    lane = lax.broadcasted_iota(jnp.int32, (blocks, TILE), 1)
+    each = TILE // groups
+    group = lane // each
+    items = cube.shape[0] // groups
+    half_rows = blocks // 2
+
+    def prepare(n, carry):
+        wanted = info[0, n, 2 * half_rows : 2 * half_rows + 1, :]
+        ids = jnp.broadcast_to(wanted, (TILE, TILE)).T
+        for part in range(cube.shape[0] // TILE):
+            places = lax.broadcasted_iota(jnp.int32, (TILE, TILE), 1) + part * TILE
+            picks[n, :, part * TILE : (part + 1) * TILE] = jnp.where(
+                ids == places.astype(jnp.float32), 1.0, 0.0
+            ).astype(jnp.bfloat16)
+        offset = jnp.concatenate([info[0, n, :half_rows], info[1, n, :half_rows]], axis=0)
+        fraction = jnp.concatenate(
+            [info[0, n, half_rows : 2 * half_rows], info[1, n, half_rows : 2 * half_rows]],
+            axis=0,
+        )
+        for b in range(groups):
+            spot = b * each + lane % each
+            start = jnp.take_along_axis(offset, spot, axis=1, mode="promise_in_bounds")
+            f = jnp.take_along_axis(fraction, spot, axis=1, mode="promise_in_bounds")
+            shifts[n, b] = start.astype(jnp.int32) + group
+            weights[n, b] = (
+                jnp.where(group == 0, -1.0 / 6.0, f + 1.0)
+                * jnp.where(group == 1, 0.5, f)
+                * jnp.where(group == 2, -0.5, f - 1.0)
+                * jnp.where(group == 3, 1.0 / 6.0, f - 2.0)
+            )
+        return carry
+
+    lax.fori_loop(0, intervals, prepare, 0)
+
+    table_copy.wait()
+    for chunk in range(CHUNKS):
+        def spec_wait(step, carry, chunk=chunk):
+            source = lax.rem(me + count - step, count)
+            spec_copy(chunk, source, source).wait_recv()
+            return carry
+
+        lax.fori_loop(1, count, spec_wait, 0)
+
+    spectra = spectra_in[...].reshape(-1, items)
+    for b in range(groups):
+        columns = pl.ds(b * per * TILE, per * TILE)
+        field = lax.dot_general(
+            spectra,
+            table[0, :, columns],
+            (((0,), (0,)), ((), ())),
+            preferred_element_type=jnp.float32,
+        ) + lax.dot_general(
+            spectra,
+            table[1, :, columns],
+            (((0,), (0,)), ((), ())),
+            preferred_element_type=jnp.float32,
+        )
+        cube[b * items : (b + 1) * items] = field.astype(jnp.bfloat16)
+
+    margin = 8
+    for d in range(per):
+        series[d, :margin] = jnp.zeros((margin, TILE), jnp.float32)
+        series[d, margin + intervals * blocks :] = jnp.zeros((margin, TILE), jnp.float32)
+
+    def sample(n, carry):
+        tiles = jnp.dot(picks[n], cube[...], preferred_element_type=jnp.float32)
+        for d in range(per):
+            terms = [
+                jnp.take_along_axis(
+                    tiles[b * blocks : (b + 1) * blocks, d * TILE : (d + 1) * TILE],
+                    shifts[n, b],
+                    axis=1,
+                    mode="promise_in_bounds",
+                )
+                * weights[n, b]
+                for b in range(groups)
+            ]
+            total = jnp.zeros((blocks, TILE), jnp.float32)
+            for k in range(groups):
+                moved = terms[(groups - 1 - k) % groups]
+                for t in range(groups - 1):
+                    moved = jnp.where(group == t, terms[(t - k) % groups], moved)
+                if k:
+                    moved = pltpu.roll(moved, TILE - k * each, 1)
+                total = total + moved
+            place = pl.ds(pl.multiple_of(margin + n * blocks, 8), blocks)
+            series[d, place] = total.astype(jnp.bfloat16).astype(jnp.float32)
+        return carry
+
+    lax.fori_loop(0, intervals, sample, 0)
+
+    def out_copy(target, source):
+        return pltpu.make_async_remote_copy(
+            src_ref=signal_out.at[target],
+            dst_ref=out_ref.at[source],
+            send_sem=out_send.at[target],
+            recv_sem=out_recv.at[source],
+            device_id=(det, target),
+            device_id_type=MESH,
+        )
+
+    def smooth(n):
+        windows = []
+        for d in range(per):
+            near = series[d, pl.ds(pl.multiple_of(n * blocks, 8), blocks + 2 * margin)]
+            windows.append(
+                jnp.concatenate(
+                    [near[margin + s : margin + s + blocks] for s in (-1, 0, 1)], axis=1
+                )
+            )
+        window = jnp.concatenate(windows, axis=0).astype(jnp.bfloat16)
+        smoothed = jnp.dot(window, band[0], preferred_element_type=jnp.float32) + jnp.dot(
+            window, band[1], preferred_element_type=jnp.float32
+        )
+        return smoothed.astype(jnp.bfloat16).reshape(per, blocks, TILE)
+
+    def finish(step, carry):
+        target = lax.rem(me + step, count)
+        signal_out[target] = smooth(target)
+        out_copy(target, me).start()
+        return carry
+
+    lax.fori_loop(1, count, finish, 0)
+    out_ref[me] = smooth(me)
+
+    def drain(step, carry):
+        target = lax.rem(me + step, count)
+        info_copy(target, me).wait_send()
+        for chunk in range(CHUNKS):
+            spec_copy(chunk, target, me).wait_send()
+        out_copy(target, me).wait_send()
+        source = lax.rem(me + count - step, count)
+        out_copy(source, source).wait_recv()
+        return carry
+
+    lax.fori_loop(1, count, drain, 0)
+    for chunk in range(CHUNKS):
+        pair_copy(chunk).wait_send()
+    share_copy.wait_send()
+
+
+def local_fused(wigner, alm, beam, crossing, offsets, fraction, taps):
+    det_count = lax.axis_size("det")
+    det = lax.axis_index("det")
+    count = lax.axis_size("ord")
+    orders, beams, lats, depth = wigner.shape
+    dets = beam.shape[0]
+    per = dets // det_count // count
+    orders_total = orders * count
+    longitudes = 2 * orders_total
+    groups = longitudes // TILE
+    items = beams * lats
+    tiles = items * groups
+    intervals = count
+    blocks = offsets.shape[1] // TILE
+    chunk_rows = orders // CHUNKS * per * 2
+
+    beam_half = lax.dynamic_slice_in_dim(beam, det * depth, depth, 2)
+    beam_pair = beam_half.reshape(det_count, -1, beams, depth)
+    beam_pair = jnp.where(det == 0, beam_pair, beam_pair[::-1]).reshape(dets, beams, depth)
+    beam_rows = jnp.repeat(jnp.transpose(beam_pair, (1, 0, 2)), 2, axis=1)
+    alm_half = lax.dynamic_slice_in_dim(alm, det * depth, depth, 2)
+    alm_rows = jnp.tile(alm_half, (1, 8, 1))
+
+    wanted = (crossing[0] % groups) * items + crossing[0] // groups
+    wanted = wanted.reshape(blocks, -1).T.reshape(1, TILE).astype(jnp.float32)
+    half = blocks // 2
+    info = jnp.concatenate(
+        [
+            lax.dynamic_slice_in_dim(
+                offsets.reshape(blocks, TILE), det * half, half, 0
+            ).astype(jnp.float32),
+            lax.dynamic_slice_in_dim(fraction.reshape(blocks, TILE), det * half, half, 0),
+            jnp.broadcast_to(wanted, (INFO_ROWS - 2 * half, TILE)),
+        ],
+        axis=0,
+    )
+    table = jnp.asarray(fourier_tables(orders_total, per))
+
+    f32, bf16 = jnp.float32, jnp.bfloat16
+    dma = pltpu.SemaphoreType.DMA
+    vmem = pl.BlockSpec(memory_space=pltpu.VMEM)
+    anywhere = pl.BlockSpec(memory_space=pl.ANY)
+    partial = pltpu.VMEM((CHUNKS, count, chunk_rows, items), f32)
+    outgoing = pltpu.VMEM((CHUNKS, count, chunk_rows, items), bf16)
+    arriving = pltpu.VMEM((count, CHUNKS, chunk_rows, items), bf16)
+    result = pl.pallas_call(
+        functools.partial(kernel, count, per, intervals, groups),
+        out_shape=jax.ShapeDtypeStruct((count, per, blocks, TILE), bf16),
+        in_specs=[
+            anywhere, vmem, vmem, anywhere, vmem,
+            pl.BlockSpec(memory_space=pltpu.SMEM),
+        ],
+        out_specs=vmem,
+        scratch_shapes=[
+            pltpu.VMEM(wigner.shape, bf16),
+            pltpu.VMEM(table.shape, bf16),
+            partial, partial, partial, outgoing, arriving,
+            pltpu.VMEM((2, count, INFO_ROWS, TILE), f32),
+            pltpu.VMEM((intervals, TILE, tiles), bf16),
+            pltpu.VMEM((intervals, groups, blocks, TILE), jnp.int32),
+            pltpu.VMEM((intervals, groups, blocks, TILE), f32),
+            pltpu.VMEM((2, 3 * TILE, TILE), bf16),
+            pltpu.VMEM((tiles, per * TILE), bf16),
+            pltpu.VMEM((per, intervals * blocks + 16, TILE), f32),
+            pltpu.VMEM((count, per, blocks, TILE), bf16),
+            dma((CHUNKS,)), dma, dma((count,)), dma((count,)), dma, dma,
+            dma((CHUNKS,)), dma((CHUNKS,)), dma((CHUNKS, count)), dma((CHUNKS, count)),
+            dma((count,)), dma((count,)),
+        ],
+        compiler_params=pltpu.CompilerParams(
+            collective_id=0, has_side_effects=True, vmem_limit_bytes=56 * 2**20
+        ),
+    )(wigner, beam_rows, alm_rows, table, info, taps)
+    return result.astype(f32).reshape(count * per, blocks * TILE)
 
 
 def with_halo(cells, sides, width):
@@ -178,19 +594,35 @@
     return smoothed.reshape(det_local, total_time)
 
 
+def splits_detectors(mesh, wigner, beam, offsets):
+    count = mesh.shape["ord"]
+    return (
+        mesh.shape["det"] == 2
+        and beam.shape[0] == 4 * count
+        and wigner.shape[0] == 4 * CHUNKS * count
+        and 2 * wigner.shape[0] == 4 * TILE
+        and wigner.shape[1:3] == (2, TILE)
+        and offsets.shape == (count, 32 * TILE)
+    )
+
+
 def solution(mesh):
-    return jax.shard_map(
-        local,
-        mesh=mesh,
-        in_specs=(
-            P("ord", None, None, "det"),
-            P("ord", None, None),
-            P(),
-            P("ord", None),
-            P("ord", None),
-            P("ord", None),
-            P(),
-        ),
-        out_specs=P("det", "ord"),
-        check_vma=False,
-    )
+    def run(wigner, alm, beam, crossing, offsets, fraction, taps):
+        fused = splits_detectors(mesh, wigner, beam, offsets)
+        return jax.shard_map(
+            local_fused if fused else local,
+            mesh=mesh,
+            in_specs=(
+                P("ord", None, None, "det"),
+                P("ord", None, None),
+                P(),
+                P("ord", None),
+                P("ord", None),
+                P("ord", None),
+                P(),
+            ),
+            out_specs=P("det", "ord"),
+            check_vma=False,
+        )(wigner, alm, beam, crossing, offsets, fraction, taps)
+
+    return run

time: 161 us -> 56.3 us (0.35)
  Pallas kernels: 0 us -> 44.8 us
  matrix products: 42.7 us -> 0 us
  starting transfers between devices: 31.1 us -> 0 us
  waiting for transfers between devices: 31 us -> 0 us
  local copies, waits for them, and re-layouts: 29.3 us -> 7.35 us
  between operations: 13.8 us -> 0.08 us
  other arithmetic: 11.2 us -> 3.74 us
    pallas_call x0 -> x1, Pallas kernels: none -> 44.8 us  [local_fused(): pl.pallas_call(functools.partial(kernel, count, per, intervals, groups),...]
    dot_general x4 -> x0, matrix products: 42.7 us -> none  [the longest x1 21.4 us: local(): jnp.einsum('jbu,uo->jbo', windows.astype(jnp.float32), banded, precision=...]
    all_to_all x5 -> x0, starting transfers between devices: 27.4 us -> none  [the longest x1 8.32 us: local(): lax.all_to_all(requests, 'ord', split_axis=0, concat_axis=0, tiled=True)]
    all_to_all x5 -> x0, waiting for transfers between devices: 26.9 us -> none  [the longest x1 13 us: local(): lax.all_to_all(result.astype(jnp.bfloat16), 'ord', split_axis=0, concat_a...]
    unnamed x34 -> x5, local copies, waits for them, and re-layouts: 12.6 us -> 2.79 us
    gather x6 -> x0, local copies, waits for them, and re-layouts: 6.05 us -> none  [the longest x1 2.21 us: local(): picked = tiles[jnp.maximum(asked, 0)]]
    ppermute x2 -> x0, waiting for transfers between devices: 4.04 us -> none  [the longest x1 4.04 us: with_halo(): lax.ppermute(head, axis, [((i + 1) % count, i) for i in range(ends)])]
    all_to_all x3 -> x0, local copies, waits for them, and re-layouts: 3.76 us -> none  [the longest x1 2.6 us: local(): lax.all_to_all(outgoing, 'ord', split_axis=1, concat_axis=2, tiled=True)]
  transfers between devices with their start and end apart: 8 -> 0, of which waited for: 5 -> 0; matrix products, arithmetic and copies ran while one was open for 15% -> 0% of each run, Pallas kernels for 0% -> 0%
where the time goes in v1:
time: 56.3 us; the launch traced here: 56 us
  Pallas kernels  44.8 us (80%)
  local copies, waits for them, and re-layouts  7.35 us (13%)
  other arithmetic  3.74 us (7%)
    pallas_call x1, Pallas kernels, local_fused(): pl.pallas_call(functools.partial(kernel, count, per, intervals, groups),...  44.8 us
    unnamed x5, local copies, waits for them, and re-layouts  2.79 us
    unnamed x2, other arithmetic  2.36 us
    another operation x2, local copies, waits for them, and re-layouts, local_fused(): alm_rows = jnp.tile(alm_half, (1, 8, 1))  1.26 us

profile of v1, /device:TPU:0, one launch (start us, length us, event | category | flops | bytes accessed | tf_op | source)
XLA Modules:
  0.0 56.0 jit_solution(11480892420084698960)
XLA Ops:
  0.0 0.0 copy-start
  0.0 1.0 %copy-done = bf16[64,2,2048]{2,1,0:T(2,128)(2,1)S(1)} copy-done((bf16[64,2,2048]{2,1,0:T(2,128)(2,1)S(1)}, bf16[64,2,2048]{2,1,0:T(2,128)(2,1)}, u32[]{:S(2)}) %copy-start) | copy-done | bytes 524312
  1.0 0.2 constant_dynamic-slice_fusion.2
  1.3 0.3 broadcast_in_dim.8
  1.6 1.0 %reshape.38.beam_ref = bf16[2,128,1024]{2,1,0:T(8,128)(2,1)} reshape(bf16[2,64,2,1024]{3,2,1,0:T(2,128)(2,1)S(1)} %broadcast_in_dim.8) | data formatting | bytes 1048576 | tf_op jit(solution)/shard_map/reshape | solution.py:370
  2.6 0.9 %constant_dynamic-slice_fusion.1 = bf16[16,2,1024]{2,1,0:T(2,128)(2,1)S(1)} fusion(bf16[16,2,2048]{2,1,0:T(2,128)(2,1)} %param.9, s32[]{:T(128)S(6)} %select_n.31), kind=kLoop, calls=%fused_computation.19 | loop fusion | bytes 131076 | tf_op jit(solution)/shard_map/dynamic_slice | solution.py:371
  3.5 0.3 tile.4
  3.8 1.0 %tile.10.alm_ref = bf16[16,16,1024]{2,1,0:T(8,128)(2,1)} reshape(bf16[16,8,2,1024]{3,2,1,0:T(2,128)(2,1)S(1)} %tile.4) | data formatting | bytes 1048576 | tf_op jit(solution)/shard_map/tile | solution.py:372
  4.8 0.6 %broadcast.31 = s32[]{:T(128)} broadcast(s32[]{:T(128)} %constant.36.clone.1), dimensions={} | broadcast | bytes 8 | tf_op args[3]
  5.4 1.4 %reduce.3 = s32[128]{0:T(128)S(1)} reduce(s32[1,128]{1,0:T(1,128)} %param.11, s32[]{:T(128)} %broadcast.31), dimensions={0}, to_apply=%param.11.reduce_sub_computation.3 | reduce | bytes 1028 | tf_op args[3]
  6.7 0.1 squeeze.4
  6.9 0.1 copy.11
  6.9 0.1 convert_element_type.21
  7.0 0.7 %constant_dynamic-slice_fusion = f32[16,128]{1,0:T(8,128)S(1)} fusion(f32[32,128]{1,0:T(8,128)} %bitcast.19, s32[]{:T(128)S(6)} %select_n.33), kind=kLoop, calls=%fused_computation.18 | loop fusion | bytes 16388 | tf_op jit(solution)/shard_map/dynamic_slice | solution.py:382
  7.7 0.7 %dynamic-slice_convert_fusion = f32[16,128]{1,0:T(8,128)S(1)} fusion(s32[32,128]{1,0:T(8,128)} %bitcast.20, s32[]{:T(128)S(6)} %select_n.33), kind=kLoop, calls=%fused_computation.17 | loop fusion | flops 2048 | bytes 16388 | tf_op jit(solution)/shard_map/convert_element_type | solution.py:381
  8.4 0.6 %pad_maximum_fusion.info_ref = f32[40,128]{1,0:T(8,128)} fusion(f32[8,128]{1,0:T(8,128)S(1)} %broadcast_in_dim.9, f32[16,128]{1,0:T(8,128)S(1)} %constant_dynamic-slice_fusion, f32[16,128]{1,0:T(8,128)S(1)} %dynamic-slice_convert_fusion), kind=kLoop, calls=%fused_computation.7 | loop fusion | flops 10240 | bytes 40960 | tf_op jit(solution)/shard_map/concatenate | solution.py:377
  9.1 44.8 %shard_map.82 = bf16[16,2,32,128]{3,2,1,0:T(8,128)(2,1)} custom-call(bf16[16,2,128,1024]{3,2,1,0:T(8,128)(2,1)} %wigner_hbm.1, bf16[2,128,1024]{2,1,0:T(8,128)(2,1)} %reshape.38.beam_ref, bf16[16,16,1024]{2,1,0:T(8,128)(2,1)} %tile.10.alm_ref, bf16[2,1024,1024]{2,1,0:T(8,128)(2,1)} %constant.47.clone.table_hbm, f32[40,128]{1,0:T(8,128)} %pad_maximum_fusion.info_ref, ...), custom_call_target="tpu_custom_call" | custom-call | tf_op jit(solution)/shard_map/pallas_call | solution.py:396
  53.9 1.0 %bitcast_convert_fusion = f32[4,8,32,128]{3,2,1,0:T(8,128)S(1)} fusion(bf16[4,8,32,128]{3,2,1,0:T(8,128)(2,1)} %bitcast.16), kind=kLoop, calls=%fused_computation.21 | loop fusion | flops 131072 | bytes 786432
  54.9 1.1 %copy.15 = f32[4,8,32,128]{3,1,2,0:T(8,128)} copy(f32[4,8,32,128]{3,2,1,0:T(8,128)S(1)} %bitcast_convert_fusion) | data formatting | bytes 1048576
  (4 shorter events, 0.1 us)
Async XLA Ops:
  0.0 1.0 %copy-start = (bf16[64,2,2048]{2,1,0:T(2,128)(2,1)S(1)}, bf16[64,2,2048]{2,1,0:T(2,128)(2,1)}, u32[]{:S(2)}) copy-start(bf16[64,2,2048]{2,1,0:T(2,128)(2,1)} %param.10) | copy-start | bytes 1572868

commit v2 on v1

--- a/solution.py
+++ b/solution.py
@@ -11,6 +11,7 @@
 
 TILE = 128
 CHUNKS = 4
+BATCH = 4
 INFO_ROWS = 40
 MESH = pl.DeviceIdType.MESH
 
@@ -39,11 +40,13 @@
 
 def kernel(
     count, per, intervals, tiles_per_item,
-    wigner_hbm, beam_ref, alm_ref, table_hbm, info_ref, taps_ref,
+    wigner_hbm, beam_hbm, alm_hbm, table_hbm, crossing_ref, offsets_ref, fraction_ref, taps_ref,
     out_ref,
+    beam_in, alm_in, beam_ref, alm_ref,
     wigner, table, partial_own, partial_out, partial_in, spectra_out, spectra_in,
-    info, picks, shifts, weights, band, cube, series, signal_out,
-    wigner_sem, table_sem, info_send, info_recv, share_send, share_recv,
+    info_ref, info, picks, shifts, weights, band, field, cube, tiles, series,
+    signal_out, signal_in,
+    small_sem, wigner_sem, table_sem, info_send, info_recv, share_send, share_recv,
     pair_send, pair_recv, spec_send, spec_recv, out_send, out_recv,
 ):
     det = lax.axis_index("det")
@@ -58,6 +61,12 @@
         part = pl.ds(chunk * chunk_orders, chunk_orders)
         return pltpu.make_async_copy(wigner_hbm.at[part], wigner.at[part], wigner_sem.at[chunk])
 
+    depth = beam_in.shape[1]
+    near_depth = pl.ds(pl.multiple_of(det * depth, TILE), depth)
+    beam_copy = pltpu.make_async_copy(beam_hbm.at[:, near_depth], beam_in, small_sem.at[0])
+    alm_copy = pltpu.make_async_copy(alm_hbm.at[:, near_depth], alm_in, small_sem.at[1])
+    beam_copy.start()
+    alm_copy.start()
     for chunk in range(CHUNKS):
         wigner_copy(chunk).start()
     table_copy = pltpu.make_async_copy(table_hbm, table, table_sem)
@@ -72,9 +81,42 @@
 
     lax.fori_loop(1, count, greet, 0)
     pl.semaphore_signal(barrier, inc=1, device_id=(partner, me), device_id_type=MESH)
-    pl.semaphore_wait(barrier, count)
-
-    info[det, me] = info_ref[...]
+
+    def select_rows(source, wanted_column):
+        chosen = jnp.where(
+            wanted_column == lax.broadcasted_iota(jnp.int32, wanted_column.shape, 1), 1.0, 0.0
+        ).astype(jnp.bfloat16)
+        return jnp.dot(chosen, source, preferred_element_type=jnp.float32).astype(jnp.bfloat16)
+
+    beams = wigner.shape[1]
+    beam_copy.wait()
+    beam_rows_all = beam_ref.shape[1]
+    row = lax.broadcasted_iota(jnp.int32, (beam_rows_all, beam_in.shape[0]), 0)
+    half_rows = beam_rows_all // 2
+    side = lax.rem(row // half_rows + det, 2)
+    beam_column = (side * (half_rows // 2) + row % half_rows // 2) * beams
+    for beam_order in range(beams):
+        beam_ref[beam_order] = select_rows(beam_in[...], beam_column + beam_order)
+    alm_copy.wait()
+    repeat = alm_ref.shape[1]
+    row = lax.broadcasted_iota(jnp.int32, (orders * repeat, alm_in.shape[0]), 0)
+    alm_ref[...] = select_rows(alm_in[...], row // repeat * 2 + row % 2).reshape(
+        alm_ref.shape
+    )
+
+    half_blocks = blocks // 2
+    near_blocks = pl.ds(pl.multiple_of(det * half_blocks, 8), half_blocks)
+    info_ref[:half_blocks] = offsets_ref[near_blocks].astype(jnp.float32)
+    info_ref[half_blocks : 2 * half_blocks] = fraction_ref[near_blocks]
+    ids = jnp.broadcast_to(crossing_ref[...], (8, TILE))
+    ids = ids % groups * (cube.shape[0] // groups) + ids // groups
+    lanes_row = lax.broadcasted_iota(jnp.int32, (8, TILE), 1)
+    info_ref[2 * half_blocks :] = jnp.take_along_axis(
+        ids.astype(jnp.float32),
+        lanes_row % blocks * groups + lanes_row // blocks,
+        axis=1,
+        mode="promise_in_bounds",
+    )
 
     def info_copy(target, source):
         return pltpu.make_async_remote_copy(
@@ -90,15 +132,12 @@
         info_copy(lax.rem(me + step, count), me).start()
         return carry
 
-    lax.fori_loop(1, count, info_start, 0)
-
     rows = per * 2
     own_rows = count * rows
 
     def product(order, beam_order):
         alm_rows = alm_ref[order]
         beam_rows = beam_ref[beam_order]
-        depth = beam_rows.shape[1]
         sky = beam_rows.reshape(-1, alm_rows.shape[0], depth) * alm_rows[None]
         return lax.dot_general(
             sky.reshape(-1, depth),
@@ -163,6 +202,10 @@
 
     for chunk in range(CHUNKS):
         multiply(chunk)
+        if chunk == 0:
+            pl.semaphore_wait(barrier, count)
+            info[det, me] = info_ref[...]
+            lax.fori_loop(1, count, info_start, 0)
         pair_copy(chunk).start()
         if chunk > 0:
             spread(chunk - 1)
@@ -242,6 +285,7 @@
     lax.fori_loop(0, intervals, prepare, 0)
 
     table_copy.wait()
+    chunk_rows = spectra_in.shape[2]
     for chunk in range(CHUNKS):
         def spec_wait(step, carry, chunk=chunk):
             source = lax.rem(me + count - step, count)
@@ -249,34 +293,40 @@
             return carry
 
         lax.fori_loop(1, count, spec_wait, 0)
-
-    spectra = spectra_in[...].reshape(-1, items)
-    for b in range(groups):
-        columns = pl.ds(b * per * TILE, per * TILE)
-        field = lax.dot_general(
-            spectra,
-            table[0, :, columns],
-            (((0,), (0,)), ((), ())),
-            preferred_element_type=jnp.float32,
-        ) + lax.dot_general(
-            spectra,
-            table[1, :, columns],
-            (((0,), (0,)), ((), ())),
-            preferred_element_type=jnp.float32,
-        )
-        cube[b * items : (b + 1) * items] = field.astype(jnp.bfloat16)
+        spectra = spectra_in[:, chunk].reshape(count * chunk_rows, items)
+        for b in range(groups):
+            columns = pl.ds(b * per * TILE, per * TILE)
+            total = sum(
+                lax.dot_general(
+                    spectra,
+                    table[part, chunk, :, columns],
+                    (((0,), (0,)), ((), ())),
+                    preferred_element_type=jnp.float32,
+                )
+                for part in range(2)
+            )
+            place = pl.ds(b * items, items)
+            if chunk > 0:
+                total = total + field[place]
+            if chunk < CHUNKS - 1:
+                field[place] = total
+            else:
+                cube[place] = total.astype(jnp.bfloat16)
 
     margin = 8
     for d in range(per):
         series[d, :margin] = jnp.zeros((margin, TILE), jnp.float32)
         series[d, margin + intervals * blocks :] = jnp.zeros((margin, TILE), jnp.float32)
 
-    def sample(n, carry):
-        tiles = jnp.dot(picks[n], cube[...], preferred_element_type=jnp.float32)
+    batch = tiles.shape[0] // TILE
+
+    def sample(first, place_in_batch):
+        n = first + place_in_batch
+        near = pl.multiple_of(place_in_batch * TILE, TILE)
         for d in range(per):
             terms = [
                 jnp.take_along_axis(
-                    tiles[b * blocks : (b + 1) * blocks, d * TILE : (d + 1) * TILE],
+                    tiles[pl.ds(near + b * blocks, blocks), d * TILE : (d + 1) * TILE],
                     shifts[n, b],
                     axis=1,
                     mode="promise_in_bounds",
@@ -294,14 +344,11 @@
                 total = total + moved
             place = pl.ds(pl.multiple_of(margin + n * blocks, 8), blocks)
             series[d, place] = total.astype(jnp.bfloat16).astype(jnp.float32)
-        return carry
-
-    lax.fori_loop(0, intervals, sample, 0)
 
     def out_copy(target, source):
         return pltpu.make_async_remote_copy(
             src_ref=signal_out.at[target],
-            dst_ref=out_ref.at[source],
+            dst_ref=signal_in.at[source],
             send_sem=out_send.at[target],
             recv_sem=out_recv.at[source],
             device_id=(det, target),
@@ -323,14 +370,47 @@
         )
         return smoothed.astype(jnp.bfloat16).reshape(per, blocks, TILE)
 
-    def finish(step, carry):
-        target = lax.rem(me + step, count)
+    def finish(target):
         signal_out[target] = smooth(target)
-        out_copy(target, me).start()
+
+        @pl.when(target != me)
+        def _():
+            out_copy(target, me).start()
+
+    batches = intervals // batch
+    origin = (me // batch + 1) * batch
+
+    def one_batch(turn, carry):
+        first = lax.rem(origin + turn * batch, intervals)
+        chosen = picks[pl.ds(first, batch)].reshape(batch * TILE, -1)
+        tiles[...] = jnp.dot(chosen, cube[...], preferred_element_type=jnp.float32)
+
+        def each_sample(step, inner):
+            sample(first, step)
+            return inner
+
+        lax.fori_loop(0, batch, each_sample, 0)
+
+        def each_finish(step, inner):
+            finish(lax.rem(first + intervals - 1 + step, intervals))
+            return inner
+
+        lax.fori_loop(jnp.where(turn == 0, 2, 0), batch, each_finish, 0)
         return carry
 
-    lax.fori_loop(1, count, finish, 0)
-    out_ref[me] = smooth(me)
+    lax.fori_loop(0, batches, one_batch, 0)
+    finish(lax.rem(origin + intervals - 1, intervals))
+    finish(lax.rem(origin, intervals))
+
+    out_ref[me] = signal_out[me].astype(jnp.float32)
+
+    def collect(step, carry):
+        source = lax.rem(me + count - step, count)
+        out_copy(source, source).wait_recv()
+        out_ref[source] = signal_in[source].astype(jnp.float32)
+        return carry
+
+    lax.fori_loop(1, count, collect, 0)
 
     def drain(step, carry):
         target = lax.rem(me + step, count)
@@ -338,8 +418,6 @@
         for chunk in range(CHUNKS):
             spec_copy(chunk, target, me).wait_send()
         out_copy(target, me).wait_send()
-        source = lax.rem(me + count - step, count)
-        out_copy(source, source).wait_recv()
         return carry
 
     lax.fori_loop(1, count, drain, 0)
@@ -350,7 +428,6 @@
 
 def local_fused(wigner, alm, beam, crossing, offsets, fraction, taps):
     det_count = lax.axis_size("det")
-    det = lax.axis_index("det")
     count = lax.axis_size("ord")
     orders, beams, lats, depth = wigner.shape
     dets = beam.shape[0]
@@ -364,27 +441,12 @@
     blocks = offsets.shape[1] // TILE
     chunk_rows = orders // CHUNKS * per * 2
 
-    beam_half = lax.dynamic_slice_in_dim(beam, det * depth, depth, 2)
-    beam_pair = beam_half.reshape(det_count, -1, beams, depth)
-    beam_pair = jnp.where(det == 0, beam_pair, beam_pair[::-1]).reshape(dets, beams, depth)
-    beam_rows = jnp.repeat(jnp.transpose(beam_pair, (1, 0, 2)), 2, axis=1)
-    alm_half = lax.dynamic_slice_in_dim(alm, det * depth, depth, 2)
-    alm_rows = jnp.tile(alm_half, (1, 8, 1))
-
-    wanted = (crossing[0] % groups) * items + crossing[0] // groups
-    wanted = wanted.reshape(blocks, -1).T.reshape(1, TILE).astype(jnp.float32)
-    half = blocks // 2
-    info = jnp.concatenate(
-        [
-            lax.dynamic_slice_in_dim(
-                offsets.reshape(blocks, TILE), det * half, half, 0
-            ).astype(jnp.float32),
-            lax.dynamic_slice_in_dim(fraction.reshape(blocks, TILE), det * half, half, 0),
-            jnp.broadcast_to(wanted, (INFO_ROWS - 2 * half, TILE)),
-        ],
-        axis=0,
-    )
-    table = jnp.asarray(fourier_tables(orders_total, per))
+    table = fourier_tables(orders_total, per).reshape(
+        2, count, CHUNKS, chunk_rows, longitudes * per
+    )
+    table = jnp.asarray(
+        np.swapaxes(table, 1, 2).reshape(2, CHUNKS, count * chunk_rows, longitudes * per)
+    )
 
     f32, bf16 = jnp.float32, jnp.bfloat16
     dma = pltpu.SemaphoreType.DMA
@@ -395,33 +457,50 @@
     arriving = pltpu.VMEM((count, CHUNKS, chunk_rows, items), bf16)
     result = pl.pallas_call(
         functools.partial(kernel, count, per, intervals, groups),
-        out_shape=jax.ShapeDtypeStruct((count, per, blocks, TILE), bf16),
+        out_shape=jax.ShapeDtypeStruct((count, per, blocks, TILE), f32),
         in_specs=[
-            anywhere, vmem, vmem, anywhere, vmem,
+            anywhere, anywhere, anywhere, anywhere, vmem, vmem, vmem,
             pl.BlockSpec(memory_space=pltpu.SMEM),
         ],
         out_specs=vmem,
         scratch_shapes=[
+            pltpu.VMEM((dets * beams, depth), bf16),
+            pltpu.VMEM((orders * 2, depth), bf16),
+            pltpu.VMEM((beams, dets * 2, depth), bf16),
+            pltpu.VMEM((orders, 16, depth), bf16),
             pltpu.VMEM(wigner.shape, bf16),
             pltpu.VMEM(table.shape, bf16),
             partial, partial, partial, outgoing, arriving,
+            pltpu.VMEM((INFO_ROWS, TILE), f32),
             pltpu.VMEM((2, count, INFO_ROWS, TILE), f32),
             pltpu.VMEM((intervals, TILE, tiles), bf16),
             pltpu.VMEM((intervals, groups, blocks, TILE), jnp.int32),
             pltpu.VMEM((intervals, groups, blocks, TILE), f32),
             pltpu.VMEM((2, 3 * TILE, TILE), bf16),
+            pltpu.VMEM((tiles, per * TILE), f32),
             pltpu.VMEM((tiles, per * TILE), bf16),
+            pltpu.VMEM((BATCH * TILE, per * TILE), f32),
             pltpu.VMEM((per, intervals * blocks + 16, TILE), f32),
             pltpu.VMEM((count, per, blocks, TILE), bf16),
-            dma((CHUNKS,)), dma, dma((count,)), dma((count,)), dma, dma,
+            pltpu.VMEM((count, per, blocks, TILE), bf16),
+            dma((2,)), dma((CHUNKS,)), dma, dma((count,)), dma((count,)), dma, dma,
             dma((CHUNKS,)), dma((CHUNKS,)), dma((CHUNKS, count)), dma((CHUNKS, count)),
             dma((count,)), dma((count,)),
         ],
         compiler_params=pltpu.CompilerParams(
             collective_id=0, has_side_effects=True, vmem_limit_bytes=56 * 2**20
         ),
-    )(wigner, beam_rows, alm_rows, table, info, taps)
-    return result.astype(f32).reshape(count * per, blocks * TILE)
+    )(
+        wigner,
+        beam.reshape(dets * beams, -1),
+        alm.reshape(orders * 2, -1),
+        table,
+        crossing,
+        offsets.reshape(blocks, TILE),
+        fraction.reshape(blocks, TILE),
+        taps,
+    )
+    return result.reshape(count * per, blocks * TILE)
 
 
 def with_halo(cells, sides, width):
@@ -603,6 +682,7 @@
         and 2 * wigner.shape[0] == 4 * TILE
         and wigner.shape[1:3] == (2, TILE)
         and offsets.shape == (count, 32 * TILE)
+        and count % BATCH == 0
     )
 
 
@@ -614,11 +694,11 @@
             mesh=mesh,
             in_specs=(
                 P("ord", None, None, "det"),
-                P("ord", None, None),
+                P("ord", None),
                 P(),
-                P("ord", None),
-                P("ord", None),
-                P("ord", None),
+                P("ord"),
+                P("ord"),
+                P("ord"),
                 P(),
             ),
             out_specs=P("det", "ord"),

time: 56.3 us -> 51.1 us (0.908)
  other arithmetic: 3.74 us -> 0 us
  local copies, waits for them, and re-layouts: 7.35 us -> 5.78 us
    reshape x1 -> x2, local copies, waits for them, and re-layouts: 0.99 us -> 3.64 us  [the longest x1 2.03 us: local_fused(): beam.reshape(dets * beams, -1)]
    unnamed x2 -> x0, other arithmetic: 2.36 us -> none
    dynamic_slice x3 -> x0, local copies, waits for them, and re-layouts: 1.77 us -> none  [the longest x1 0.89 us: local_fused(): alm_half = lax.dynamic_slice_in_dim(alm, det * depth, depth, 2)]
    another operation x2 -> x0, local copies, waits for them, and re-layouts: 1.26 us -> none  [local_fused(): alm_rows = jnp.tile(alm_half, (1, 8, 1))]
    convert_element_type x2 -> x0, other arithmetic: 0.73 us -> none  [the longest x1 0.7 us: local_fused(): info = jnp.concatenate([lax.dynamic_slice_in_dim(offsets.reshape(blocks,...]
    unnamed x5 -> x1, local copies, waits for them, and re-layouts: 2.79 us -> 2.14 us
    concatenate x1 -> x0, other arithmetic: 0.6 us -> none  [local_fused(): jnp.concatenate([lax.dynamic_slice_in_dim(offsets.reshape(blocks, TILE),...]
where the time goes in v2:
time: 51.1 us; the launch traced here: 50.9 us
  Pallas kernels  45.1 us (88%)
  local copies, waits for them, and re-layouts  5.78 us (11%)
    pallas_call x1, Pallas kernels, local_fused(): pl.pallas_call(functools.partial(kernel, count, per, intervals, groups),...  45.1 us
    unnamed x1, local copies, waits for them, and re-layouts  2.14 us
    reshape x1, local copies, waits for them, and re-layouts, local_fused(): beam.reshape(dets * beams, -1)  2.03 us
    reshape x1, local copies, waits for them, and re-layouts, local_fused(): alm.reshape(orders * 2, -1)  1.61 us

profile of v2, /device:TPU:0, one launch (start us, length us, event | category | flops | bytes accessed | tf_op | source)
XLA Modules:
  0.0 50.9 jit_solution(12461974810583635242)
XLA Ops:
  0.0 1.6 %reshape.16.alm_hbm = bf16[32,2048]{1,0:T(8,128)(2,1)} reshape(bf16[16,2,2048]{2,1,0:T(2,128)(2,1)} %param.9) | data formatting | bytes 262144 | tf_op jit(solution)/shard_map/reshape | solution.py:496
  1.6 2.0 %reshape.15.beam_hbm = bf16[128,2048]{1,0:T(8,128)(2,1)} reshape(bf16[64,2,2048]{2,1,0:T(2,128)(2,1)} %param.10) | data formatting | bytes 1048576 | tf_op jit(solution)/shard_map/reshape | solution.py:495
  3.6 45.1 %shard_map.82 = f32[16,2,32,128]{3,2,1,0:T(8,128)} custom-call(bf16[16,2,128,1024]{3,2,1,0:T(8,128)(2,1)} %wigner_hbm.1, bf16[128,2048]{1,0:T(8,128)(2,1)} %reshape.15.beam_hbm, bf16[32,2048]{1,0:T(8,128)(2,1)} %reshape.16.alm_hbm, bf16[2,4,256,1024]{3,2,1,0:T(8,128)(2,1)} %constant.2.clone.table_hbm, s32[1,128]{1,0:T(1,128)} %crossing_ref.1, ...), custom_call_target="tpu_custom_call" | custom-call | tf_op jit(solution)/shard_map/pallas_call | solution.py:458
  48.7 2.1 %copy.11 = f32[4,8,32,128]{3,1,2,0:T(8,128)} copy(f32[4,8,32,128]{3,2,1,0:T(8,128)} %bitcast.7) | data formatting | bytes 1048576

commit v3 on v2

--- a/solution.py
+++ b/solution.py
@@ -11,6 +11,7 @@
 
 TILE = 128
 CHUNKS = 4
+PLANE = 4
 BATCH = 4
 INFO_ROWS = 40
 MESH = pl.DeviceIdType.MESH
@@ -46,7 +47,7 @@
     wigner, table, partial_own, partial_out, partial_in, spectra_out, spectra_in,
     info_ref, info, picks, shifts, weights, band, field, cube, tiles, series,
     signal_out, signal_in,
-    small_sem, wigner_sem, table_sem, info_send, info_recv, share_send, share_recv,
+    small_sem, wigner_sem, table_sem, info_send, info_recv, column_send, column_recv, share_send, share_recv,
     pair_send, pair_recv, spec_send, spec_recv, out_send, out_recv,
 ):
     det = lax.axis_index("det")
@@ -61,10 +62,10 @@
         part = pl.ds(chunk * chunk_orders, chunk_orders)
         return pltpu.make_async_copy(wigner_hbm.at[part], wigner.at[part], wigner_sem.at[chunk])
 
-    depth = beam_in.shape[1]
+    depth = beam_in.shape[2]
     near_depth = pl.ds(pl.multiple_of(det * depth, TILE), depth)
-    beam_copy = pltpu.make_async_copy(beam_hbm.at[:, near_depth], beam_in, small_sem.at[0])
-    alm_copy = pltpu.make_async_copy(alm_hbm.at[:, near_depth], alm_in, small_sem.at[1])
+    beam_copy = pltpu.make_async_copy(beam_hbm.at[:, :, near_depth], beam_in, small_sem.at[0])
+    alm_copy = pltpu.make_async_copy(alm_hbm.at[:, :, near_depth], alm_in, small_sem.at[1])
     beam_copy.start()
     alm_copy.start()
     for chunk in range(CHUNKS):
@@ -91,16 +92,18 @@
     beams = wigner.shape[1]
     beam_copy.wait()
     beam_rows_all = beam_ref.shape[1]
-    row = lax.broadcasted_iota(jnp.int32, (beam_rows_all, beam_in.shape[0]), 0)
+    beam_source = beam_in[...].reshape(-1, depth)
+    row = lax.broadcasted_iota(jnp.int32, (beam_rows_all, beam_source.shape[0]), 0)
     half_rows = beam_rows_all // 2
     side = lax.rem(row // half_rows + det, 2)
     beam_column = (side * (half_rows // 2) + row % half_rows // 2) * beams
     for beam_order in range(beams):
-        beam_ref[beam_order] = select_rows(beam_in[...], beam_column + beam_order)
+        beam_ref[beam_order] = select_rows(beam_source, beam_column + beam_order)
     alm_copy.wait()
     repeat = alm_ref.shape[1]
-    row = lax.broadcasted_iota(jnp.int32, (orders * repeat, alm_in.shape[0]), 0)
-    alm_ref[...] = select_rows(alm_in[...], row // repeat * 2 + row % 2).reshape(
+    alm_source = alm_in[...].reshape(-1, depth)
+    row = lax.broadcasted_iota(jnp.int32, (orders * repeat, alm_source.shape[0]), 0)
+    alm_ref[...] = select_rows(alm_source, row // repeat * 2 + row % 2).reshape(
         alm_ref.shape
     )
 
@@ -118,19 +121,31 @@
         mode="promise_in_bounds",
     )
 
-    def info_copy(target, source):
+    planes = count // PLANE
+    near, plane = lax.rem(me, PLANE), me // PLANE
+
+    def info_copy(step):
         return pltpu.make_async_remote_copy(
             src_ref=info_ref,
-            dst_ref=info.at[det, source],
-            send_sem=info_send.at[target],
-            recv_sem=info_recv.at[source],
-            device_id=(det, target),
+            dst_ref=info.at[det, near, plane],
+            send_sem=info_send,
+            recv_sem=info_recv,
+            device_id=(det, lax.rem(me + step * PLANE, count)),
             device_id_type=MESH,
         )
 
-    def info_start(step, carry):
-        info_copy(lax.rem(me + step, count), me).start()
-        return carry
+    def column_copy(step):
+        return pltpu.make_async_remote_copy(
+            src_ref=info.at[det, near],
+            dst_ref=info.at[det, near],
+            send_sem=column_send,
+            recv_sem=column_recv,
+            device_id=(det, plane * PLANE + lax.rem(near + step, PLANE)),
+            device_id_type=MESH,
+        )
+
+    def await_bytes(block, semaphore):
+        pltpu.make_async_copy(block, block, semaphore).wait()
 
     rows = per * 2
     own_rows = count * rows
@@ -182,8 +197,8 @@
         return pltpu.make_async_remote_copy(
             src_ref=spectra_out.at[chunk, target],
             dst_ref=spectra_in.at[source, chunk],
-            send_sem=spec_send.at[chunk, target],
-            recv_sem=spec_recv.at[chunk, source],
+            send_sem=spec_send.at[chunk],
+            recv_sem=spec_recv.at[chunk],
             device_id=(det, target),
             device_id_type=MESH,
         )
@@ -193,30 +208,27 @@
         total = (partial_own[chunk] + partial_in[chunk]).astype(jnp.bfloat16)
         spectra_out[chunk] = total
 
-        def start(step, carry):
-            spec_copy(chunk, lax.rem(me + step, count), me).start()
-            return carry
-
-        lax.fori_loop(1, count, start, 0)
+        for step in range(count - 1):
+            spec_copy(chunk, lax.rem(me + 1 + (step + PLANE - 1) % (count - 1), count), me).start()
         spectra_in[me, chunk] = spectra_out[chunk, me]
 
     for chunk in range(CHUNKS):
         multiply(chunk)
         if chunk == 0:
             pl.semaphore_wait(barrier, count)
-            info[det, me] = info_ref[...]
-            lax.fori_loop(1, count, info_start, 0)
+            info[det, near, plane] = info_ref[...]
+            for step in range(1, planes):
+                info_copy(step).start()
         pair_copy(chunk).start()
         if chunk > 0:
             spread(chunk - 1)
+        if chunk == CHUNKS // 2:
+            await_bytes(info.at[det, near, pl.ds(0, planes - 1)], info_recv)
+            for step in range(1, PLANE):
+                column_copy(step).start()
     spread(CHUNKS - 1)
 
-    def info_wait(step, carry):
-        source = lax.rem(me + count - step, count)
-        info_copy(source, source).wait_recv()
-        return carry
-
-    lax.fori_loop(1, count, info_wait, 0)
+    await_bytes(info.at[det, pl.ds(0, PLANE - 1)], column_recv)
     share_copy = pltpu.make_async_remote_copy(
         src_ref=info.at[det],
         dst_ref=info.at[det],
@@ -227,19 +239,19 @@
     )
     share_copy.start()
 
-    shape = (3 * TILE, TILE)
-    lag = (
-        lax.broadcasted_iota(jnp.int32, shape, 0) - lax.broadcasted_iota(jnp.int32, shape, 1)
-    )
+    shape = (2 * TILE, TILE)
+    place = lax.broadcasted_iota(jnp.int32, shape, 0)
+    place = jnp.where(place < 3 * TILE // 2, place, place - 2 * TILE)
+    lag = place - lax.broadcasted_iota(jnp.int32, shape, 1)
     reach = taps_ref.shape[0] // 2
 
     def add_tap(place, total):
-        return jnp.where(lag == place + (TILE - reach), taps_ref[place], total)
+        return jnp.where(lag == place - reach, taps_ref[place], total)
 
     band_values = lax.fori_loop(0, taps_ref.shape[0], add_tap, jnp.zeros(shape, jnp.float32))
     band_high, band_low = split_parts(band_values)
-    band[0] = band_high
-    band[1] = band_low
+    band[:, :TILE] = band_high
+    band[:, TILE:] = band_low
 
     pltpu.make_async_remote_copy(
         src_ref=info.at[partner],
@@ -257,16 +269,16 @@
     half_rows = blocks // 2
 
     def prepare(n, carry):
-        wanted = info[0, n, 2 * half_rows : 2 * half_rows + 1, :]
+        wanted = info[0, n % PLANE, n // PLANE, 2 * half_rows : 2 * half_rows + 1, :]
         ids = jnp.broadcast_to(wanted, (TILE, TILE)).T
         for part in range(cube.shape[0] // TILE):
             places = lax.broadcasted_iota(jnp.int32, (TILE, TILE), 1) + part * TILE
             picks[n, :, part * TILE : (part + 1) * TILE] = jnp.where(
                 ids == places.astype(jnp.float32), 1.0, 0.0
             ).astype(jnp.bfloat16)
-        offset = jnp.concatenate([info[0, n, :half_rows], info[1, n, :half_rows]], axis=0)
+        offset = jnp.concatenate([info[0, n % PLANE, n // PLANE, :half_rows], info[1, n % PLANE, n // PLANE, :half_rows]], axis=0)
         fraction = jnp.concatenate(
-            [info[0, n, half_rows : 2 * half_rows], info[1, n, half_rows : 2 * half_rows]],
+            [info[0, n % PLANE, n // PLANE, half_rows : 2 * half_rows], info[1, n % PLANE, n // PLANE, half_rows : 2 * half_rows]],
             axis=0,
         )
         for b in range(groups):
@@ -287,12 +299,7 @@
     table_copy.wait()
     chunk_rows = spectra_in.shape[2]
     for chunk in range(CHUNKS):
-        def spec_wait(step, carry, chunk=chunk):
-            source = lax.rem(me + count - step, count)
-            spec_copy(chunk, source, source).wait_recv()
-            return carry
-
-        lax.fori_loop(1, count, spec_wait, 0)
+        await_bytes(spectra_in.at[pl.ds(0, count - 1), chunk], spec_recv.at[chunk])
         spectra = spectra_in[:, chunk].reshape(count * chunk_rows, items)
         for b in range(groups):
             columns = pl.ds(b * per * TILE, per * TILE)
@@ -349,7 +356,7 @@
         return pltpu.make_async_remote_copy(
             src_ref=signal_out.at[target],
             dst_ref=signal_in.at[source],
-            send_sem=out_send.at[target],
+            send_sem=out_send,
             recv_sem=out_recv.at[source],
             device_id=(det, target),
             device_id_type=MESH,
@@ -358,16 +365,15 @@
     def smooth(n):
         windows = []
         for d in range(per):
-            near = series[d, pl.ds(pl.multiple_of(n * blocks, 8), blocks + 2 * margin)]
-            windows.append(
-                jnp.concatenate(
-                    [near[margin + s : margin + s + blocks] for s in (-1, 0, 1)], axis=1
-                )
+            rows_near = series[d, pl.ds(pl.multiple_of(n * blocks, 8), blocks + 2 * margin)]
+            before, here, after = (
+                rows_near[margin + s : margin + s + blocks] for s in (-1, 0, 1)
             )
+            sides = jnp.where(lane < TILE // 2, after, before)
+            windows.append(jnp.concatenate([here, sides], axis=1))
         window = jnp.concatenate(windows, axis=0).astype(jnp.bfloat16)
-        smoothed = jnp.dot(window, band[0], preferred_element_type=jnp.float32) + jnp.dot(
-            window, band[1], preferred_element_type=jnp.float32
-        )
+        both = jnp.dot(window, band[...], preferred_element_type=jnp.float32)
+        smoothed = both[:, :TILE] + both[:, TILE:]
         return smoothed.astype(jnp.bfloat16).reshape(per, blocks, TILE)
 
     def finish(target):
@@ -402,25 +408,25 @@
     finish(lax.rem(origin + intervals - 1, intervals))
     finish(lax.rem(origin, intervals))
 
-    out_ref[me] = signal_out[me].astype(jnp.float32)
-
-    def collect(step, carry):
-        source = lax.rem(me + count - step, count)
-        out_copy(source, source).wait_recv()
-        out_ref[source] = signal_in[source].astype(jnp.float32)
-        return carry
-
-    lax.fori_loop(1, count, collect, 0)
-
-    def drain(step, carry):
-        target = lax.rem(me + step, count)
-        info_copy(target, me).wait_send()
-        for chunk in range(CHUNKS):
-            spec_copy(chunk, target, me).wait_send()
-        out_copy(target, me).wait_send()
-        return carry
-
-    lax.fori_loop(1, count, drain, 0)
+    signal_in[me] = signal_out[me]
+    for source in range(count):
+        @pl.when(source != me)
+        def _(source=source):
+            out_copy(source, source).wait_recv()
+
+        for d in range(per):
+            values = signal_in[source, d].astype(jnp.float32)
+            row = source * per + d
+            for block in range(blocks):
+                out_ref[row : row + 1, block * TILE : (block + 1) * TILE] = values[
+                    block : block + 1
+                ]
+
+    await_bytes(info.at[det, near, pl.ds(0, planes - 1)], info_send)
+    await_bytes(info.at[det, pl.ds(0, PLANE - 1)], column_send)
+    await_bytes(signal_out.at[pl.ds(0, count - 1)], out_send)
+    for chunk in range(CHUNKS):
+        await_bytes(spectra_out.at[chunk, pl.ds(0, count - 1)], spec_send.at[chunk])
     for chunk in range(CHUNKS):
         pair_copy(chunk).wait_send()
     share_copy.wait_send()
@@ -457,50 +463,50 @@
     arriving = pltpu.VMEM((count, CHUNKS, chunk_rows, items), bf16)
     result = pl.pallas_call(
         functools.partial(kernel, count, per, intervals, groups),
-        out_shape=jax.ShapeDtypeStruct((count, per, blocks, TILE), f32),
+        out_shape=jax.ShapeDtypeStruct((count * per, blocks * TILE), f32),
         in_specs=[
             anywhere, anywhere, anywhere, anywhere, vmem, vmem, vmem,
             pl.BlockSpec(memory_space=pltpu.SMEM),
         ],
         out_specs=vmem,
         scratch_shapes=[
-            pltpu.VMEM((dets * beams, depth), bf16),
-            pltpu.VMEM((orders * 2, depth), bf16),
+            pltpu.VMEM((dets, beams, depth), bf16),
+            pltpu.VMEM((orders, 2, depth), bf16),
             pltpu.VMEM((beams, dets * 2, depth), bf16),
             pltpu.VMEM((orders, 16, depth), bf16),
             pltpu.VMEM(wigner.shape, bf16),
             pltpu.VMEM(table.shape, bf16),
             partial, partial, partial, outgoing, arriving,
             pltpu.VMEM((INFO_ROWS, TILE), f32),
-            pltpu.VMEM((2, count, INFO_ROWS, TILE), f32),
+            pltpu.VMEM((2, PLANE, count // PLANE, INFO_ROWS, TILE), f32),
             pltpu.VMEM((intervals, TILE, tiles), bf16),
             pltpu.VMEM((intervals, groups, blocks, TILE), jnp.int32),
             pltpu.VMEM((intervals, groups, blocks, TILE), f32),
-            pltpu.VMEM((2, 3 * TILE, TILE), bf16),
+            pltpu.VMEM((2 * TILE, 2 * TILE), bf16),
             pltpu.VMEM((tiles, per * TILE), f32),
             pltpu.VMEM((tiles, per * TILE), bf16),
             pltpu.VMEM((BATCH * TILE, per * TILE), f32),
             pltpu.VMEM((per, intervals * blocks + 16, TILE), f32),
             pltpu.VMEM((count, per, blocks, TILE), bf16),
             pltpu.VMEM((count, per, blocks, TILE), bf16),
-            dma((2,)), dma((CHUNKS,)), dma, dma((count,)), dma((count,)), dma, dma,
-            dma((CHUNKS,)), dma((CHUNKS,)), dma((CHUNKS, count)), dma((CHUNKS, count)),
-            dma((count,)), dma((count,)),
+            dma((2,)), dma((CHUNKS,)), dma, dma, dma, dma, dma, dma, dma,
+            dma((CHUNKS,)), dma((CHUNKS,)), dma((CHUNKS,)), dma((CHUNKS,)),
+            dma, dma((count,)),
         ],
         compiler_params=pltpu.CompilerParams(
             collective_id=0, has_side_effects=True, vmem_limit_bytes=56 * 2**20
         ),
     )(
         wigner,
-        beam.reshape(dets * beams, -1),
-        alm.reshape(orders * 2, -1),
+        beam,
+        alm,
         table,
         crossing,
         offsets.reshape(blocks, TILE),
         fraction.reshape(blocks, TILE),
         taps,
     )
-    return result.reshape(count * per, blocks * TILE)
+    return result
 
 
 def with_halo(cells, sides, width):
@@ -683,6 +689,7 @@
         and wigner.shape[1:3] == (2, TILE)
         and offsets.shape == (count, 32 * TILE)
         and count % BATCH == 0
+        and count % PLANE == 0
     )
 
 

time: 51.1 us -> 41.5 us (0.81)
  Pallas kernels: 45.1 us -> 39.3 us
  local copies, waits for them, and re-layouts: 5.78 us -> 1.87 us
    pallas_call x1, Pallas kernels: 45.1 us -> 39.3 us  [local_fused(): pl.pallas_call(functools.partial(kernel, count, per, intervals, groups),...]
    reshape x2 -> x0, local copies, waits for them, and re-layouts: 3.64 us -> none  [the longest x1 2.03 us: local_fused(): beam.reshape(dets * beams, -1)]
where the time goes in v3:
time: 41.5 us; the launch traced here: 41.2 us
  Pallas kernels  39.3 us (95%)
  local copies, waits for them, and re-layouts  1.87 us (5%)
    pallas_call x1, Pallas kernels, local_fused(): pl.pallas_call(functools.partial(kernel, count, per, intervals, groups),...  39.3 us
    unnamed x1, local copies, waits for them, and re-layouts  1.87 us

profile of v3, /device:TPU:0, one launch (start us, length us, event | category | flops | bytes accessed | tf_op | source)
XLA Modules:
  0.0 41.2 jit_solution(8513755415464621982)
XLA Ops:
  0.0 39.3 %shard_map.82 = f32[32,4096]{1,0:T(8,128)} custom-call(bf16[16,2,128,1024]{3,2,1,0:T(8,128)(2,1)} %wigner_hbm.1, bf16[64,2,2048]{2,1,0:T(2,128)(2,1)} %beam_hbm.1, bf16[16,2,2048]{2,1,0:T(2,128)(2,1)} %alm_hbm.1, bf16[2,4,256,1024]{3,2,1,0:T(8,128)(2,1)} %constant.2.clone.table_hbm, s32[1,128]{1,0:T(1,128)} %crossing_ref.1, s32[32,128]{1,0:T(8,128)} %bitcast.2, ...), custom_call_target="tpu_custom_call" | custom-call | tf_op jit(solution)/shard_map/pallas_call | solution.py:464
  39.4 1.9 %copy.10 = f32[32,4096]{1,0:T(8,128)} copy(f32[32,4096]{1,0:T(8,128)} %shard_map.82) | data formatting | bytes 1048576

commit v4 on v3

--- a/solution.py
+++ b/solution.py
@@ -46,7 +46,7 @@
     beam_in, alm_in, beam_ref, alm_ref,
     wigner, table, partial_own, partial_out, partial_in, spectra_out, spectra_in,
     info_ref, info, picks, shifts, weights, band, field, cube, tiles, series,
-    signal_out, signal_in,
+    signal_out, signal_in, wide,
     small_sem, wigner_sem, table_sem, info_send, info_recv, column_send, column_recv, share_send, share_recv,
     pair_send, pair_recv, spec_send, spec_recv, out_send, out_recv,
 ):
@@ -181,7 +181,7 @@
                     )
             return carry
 
-        lax.fori_loop(0, chunk_orders // 2, pair, 0)
+        lax.fori_loop(0, chunk_orders // 2, pair, 0, unroll=True)
 
     def pair_copy(chunk):
         return pltpu.make_async_remote_copy(
@@ -357,28 +357,29 @@
             src_ref=signal_out.at[target],
             dst_ref=signal_in.at[source],
             send_sem=out_send,
-            recv_sem=out_recv.at[source],
+            recv_sem=out_recv,
             device_id=(det, target),
             device_id_type=MESH,
         )
 
-    def smooth(n):
+    def smooth(targets):
         windows = []
-        for d in range(per):
-            rows_near = series[d, pl.ds(pl.multiple_of(n * blocks, 8), blocks + 2 * margin)]
-            before, here, after = (
-                rows_near[margin + s : margin + s + blocks] for s in (-1, 0, 1)
-            )
-            sides = jnp.where(lane < TILE // 2, after, before)
-            windows.append(jnp.concatenate([here, sides], axis=1))
+        for n in targets:
+            for d in range(per):
+                rows_near = series[d, pl.ds(pl.multiple_of(n * blocks, 8), blocks + 2 * margin)]
+                before, here, after = (
+                    rows_near[margin + s : margin + s + blocks] for s in (-1, 0, 1)
+                )
+                sides = jnp.where(lane < TILE // 2, after, before)
+                windows.append(jnp.concatenate([here, sides], axis=1))
         window = jnp.concatenate(windows, axis=0).astype(jnp.bfloat16)
         both = jnp.dot(window, band[...], preferred_element_type=jnp.float32)
-        smoothed = both[:, :TILE] + both[:, TILE:]
-        return smoothed.astype(jnp.bfloat16).reshape(per, blocks, TILE)
-
-    def finish(target):
-        signal_out[target] = smooth(target)
-
+        smoothed = (both[:, :TILE] + both[:, TILE:]).astype(jnp.bfloat16)
+        smoothed = smoothed.reshape(len(targets), per, blocks, TILE)
+        for place, n in enumerate(targets):
+            signal_out[n] = smoothed[place]
+
+    def send(target):
         @pl.when(target != me)
         def _():
             out_copy(target, me).start()
@@ -390,37 +391,42 @@
         first = lax.rem(origin + turn * batch, intervals)
         chosen = picks[pl.ds(first, batch)].reshape(batch * TILE, -1)
         tiles[...] = jnp.dot(chosen, cube[...], preferred_element_type=jnp.float32)
-
-        def each_sample(step, inner):
+        for step in range(batch):
             sample(first, step)
-            return inner
-
-        lax.fori_loop(0, batch, each_sample, 0)
-
-        def each_finish(step, inner):
-            finish(lax.rem(first + intervals - 1 + step, intervals))
-            return inner
-
-        lax.fori_loop(jnp.where(turn == 0, 2, 0), batch, each_finish, 0)
+        targets = [lax.rem(first + intervals - 1 + step, intervals) for step in range(batch)]
+
+        @pl.when(turn == 0)
+        def _():
+            smooth(targets[2:])
+
+        @pl.when(turn > 0)
+        def _():
+            smooth(targets)
+            for target in targets[:2]:
+                send(target)
+
+        for target in targets[2:]:
+            send(target)
         return carry
 
     lax.fori_loop(0, batches, one_batch, 0)
-    finish(lax.rem(origin + intervals - 1, intervals))
-    finish(lax.rem(origin, intervals))
+    targets = [lax.rem(origin + intervals - 1 + step, intervals) for step in range(2)]
+    smooth(targets)
+    for target in targets:
+        send(target)
 
     signal_in[me] = signal_out[me]
-    for source in range(count):
-        @pl.when(source != me)
-        def _(source=source):
-            out_copy(source, source).wait_recv()
-
-        for d in range(per):
-            values = signal_in[source, d].astype(jnp.float32)
-            row = source * per + d
-            for block in range(blocks):
-                out_ref[row : row + 1, block * TILE : (block + 1) * TILE] = values[
-                    block : block + 1
-                ]
+    await_bytes(signal_in.at[pl.ds(0, count - 1)], out_recv)
+    wide[...] = signal_in[...].astype(jnp.float32).reshape(wide.shape)
+    rows_out = out_ref.shape[0]
+    for block in range(blocks):
+        parts = [
+            wide[pl.ds(first * blocks + block, 8, stride=blocks), :]
+            for first in range(0, rows_out, 8)
+        ]
+        out_ref[:, block * TILE : (block + 1) * TILE] = jnp.concatenate(parts, axis=0).astype(
+            out_ref.dtype
+        )
 
     await_bytes(info.at[det, near, pl.ds(0, planes - 1)], info_send)
     await_bytes(info.at[det, pl.ds(0, PLANE - 1)], column_send)
@@ -463,7 +469,7 @@
     arriving = pltpu.VMEM((count, CHUNKS, chunk_rows, items), bf16)
     result = pl.pallas_call(
         functools.partial(kernel, count, per, intervals, groups),
-        out_shape=jax.ShapeDtypeStruct((count * per, blocks * TILE), f32),
+        out_shape=jax.ShapeDtypeStruct((count * per, blocks * TILE), bf16),
         in_specs=[
             anywhere, anywhere, anywhere, anywhere, vmem, vmem, vmem,
             pl.BlockSpec(memory_space=pltpu.SMEM),
@@ -489,9 +495,10 @@
             pltpu.VMEM((per, intervals * blocks + 16, TILE), f32),
             pltpu.VMEM((count, per, blocks, TILE), bf16),
             pltpu.VMEM((count, per, blocks, TILE), bf16),
+            pltpu.VMEM((count * per * blocks, TILE), f32),
             dma((2,)), dma((CHUNKS,)), dma, dma, dma, dma, dma, dma, dma,
             dma((CHUNKS,)), dma((CHUNKS,)), dma((CHUNKS,)), dma((CHUNKS,)),
-            dma, dma((count,)),
+            dma, dma,
         ],
         compiler_params=pltpu.CompilerParams(
             collective_id=0, has_side_effects=True, vmem_limit_bytes=56 * 2**20
@@ -506,7 +513,7 @@
         fraction.reshape(blocks, TILE),
         taps,
     )
-    return result
+    return result.astype(f32)
 
 
 def with_halo(cells, sides, width):

time: 41.5 us -> 38.2 us (0.920)
  Pallas kernels: 39.3 us -> 36.2 us
  local copies, waits for them, and re-layouts: 1.87 us -> 0 us
  other arithmetic: 0 us -> 1.78 us
    pallas_call x1, Pallas kernels: 39.3 us -> 36.2 us  [local_fused(): pl.pallas_call(functools.partial(kernel, count, per, intervals, groups),...]
    unnamed x1 -> x0, local copies, waits for them, and re-layouts: 1.87 us -> none
    convert_element_type x0 -> x1, other arithmetic: none -> 1.78 us  [local_fused(): return result.astype(f32)]
where the time goes in v4:
time: 38.2 us; the launch traced here: 38 us
  Pallas kernels  36.2 us (95%)
  other arithmetic  1.78 us (5%)
    pallas_call x1, Pallas kernels, local_fused(): pl.pallas_call(functools.partial(kernel, count, per, intervals, groups),...  36.2 us
    convert_element_type x1, other arithmetic, local_fused(): return result.astype(f32)  1.78 us

profile of v4, /device:TPU:0, one launch (start us, length us, event | category | flops | bytes accessed | tf_op | source)
XLA Modules:
  0.0 38.0 jit_solution(11788983612786030820)
XLA Ops:
  0.0 36.2 %shard_map.82 = bf16[32,4096]{1,0:T(8,128)(2,1)} custom-call(bf16[16,2,128,1024]{3,2,1,0:T(8,128)(2,1)} %wigner_hbm.1, bf16[64,2,2048]{2,1,0:T(2,128)(2,1)} %beam_hbm.1, bf16[16,2,2048]{2,1,0:T(2,128)(2,1)} %alm_hbm.1, bf16[2,4,256,1024]{3,2,1,0:T(8,128)(2,1)} %constant.2.clone.table_hbm, s32[1,128]{1,0:T(1,128)} %crossing_ref.1, s32[32,128]{1,0:T(8,128)} %bitcast.2, ...), custom_call_target="tpu_custom_call" | custom-call | tf_op jit(solution)/shard_map/pallas_call | solution.py:470
  36.2 1.8 %convert_element_type.3 = f32[32,4096]{1,0:T(8,128)} convert(bf16[32,4096]{1,0:T(8,128)(2,1)} %shard_map.82) | non-fusion elementwise | flops 131072 | bytes 786432 | tf_op jit(solution)/shard_map/convert_element_type | solution.py:516

commit v5 on v4

--- a/solution.py
+++ b/solution.py
@@ -46,7 +46,7 @@
     beam_in, alm_in, beam_ref, alm_ref,
     wigner, table, partial_own, partial_out, partial_in, spectra_out, spectra_in,
     info_ref, info, picks, shifts, weights, band, field, cube, tiles, series,
-    signal_out, signal_in, wide,
+    signal_out,
     small_sem, wigner_sem, table_sem, info_send, info_recv, column_send, column_recv, share_send, share_recv,
     pair_send, pair_recv, spec_send, spec_recv, out_send, out_recv,
 ):
@@ -164,9 +164,9 @@
     def multiply(chunk):
         wigner_copy(chunk).wait()
 
-        def pair(step, carry):
+        def pair(step):
             first = chunk * chunk_orders + 2 * step
-            place = pl.ds(pl.multiple_of(step * 2 * rows, 2 * rows), 2 * rows)
+            place = pl.ds(step * 2 * rows, 2 * rows)
             for beam_order in range(wigner.shape[1]):
                 lanes = pl.ds(beam_order * wigner.shape[2], wigner.shape[2])
                 one = product(first, beam_order)
@@ -179,9 +179,11 @@
                         ],
                         axis=1,
                     )
-            return carry
-
-        lax.fori_loop(0, chunk_orders // 2, pair, 0, unroll=True)
+
+        for step in range(chunk_orders // 2):
+            pair(step)
+            if step == 0 and chunk > 0:
+                spread(chunk - 1)
 
     def pair_copy(chunk):
         return pltpu.make_async_remote_copy(
@@ -220,8 +222,6 @@
             for step in range(1, planes):
                 info_copy(step).start()
         pair_copy(chunk).start()
-        if chunk > 0:
-            spread(chunk - 1)
         if chunk == CHUNKS // 2:
             await_bytes(info.at[det, near, pl.ds(0, planes - 1)], info_recv)
             for step in range(1, PLANE):
@@ -268,13 +268,14 @@
     items = cube.shape[0] // groups
     half_rows = blocks // 2
 
+    places = lax.broadcasted_iota(jnp.int32, (TILE, TILE), 1).astype(jnp.float32)
+
     def prepare(n, carry):
         wanted = info[0, n % PLANE, n // PLANE, 2 * half_rows : 2 * half_rows + 1, :]
         ids = jnp.broadcast_to(wanted, (TILE, TILE)).T
         for part in range(cube.shape[0] // TILE):
-            places = lax.broadcasted_iota(jnp.int32, (TILE, TILE), 1) + part * TILE
             picks[n, :, part * TILE : (part + 1) * TILE] = jnp.where(
-                ids == places.astype(jnp.float32), 1.0, 0.0
+                ids - part * TILE == places, 1.0, 0.0
             ).astype(jnp.bfloat16)
         offset = jnp.concatenate([info[0, n % PLANE, n // PLANE, :half_rows], info[1, n % PLANE, n // PLANE, :half_rows]], axis=0)
         fraction = jnp.concatenate(
@@ -294,21 +295,19 @@
             )
         return carry
 
-    lax.fori_loop(0, intervals, prepare, 0)
+    lax.fori_loop(0, intervals, prepare, 0, unroll=2)
 
     table_copy.wait()
     chunk_rows = spectra_in.shape[2]
     for chunk in range(CHUNKS):
         await_bytes(spectra_in.at[pl.ds(0, count - 1), chunk], spec_recv.at[chunk])
         spectra = spectra_in[:, chunk].reshape(count * chunk_rows, items)
+        turned = spectra.T
         for b in range(groups):
             columns = pl.ds(b * per * TILE, per * TILE)
             total = sum(
-                lax.dot_general(
-                    spectra,
-                    table[part, chunk, :, columns],
-                    (((0,), (0,)), ((), ())),
-                    preferred_element_type=jnp.float32,
+                jnp.dot(
+                    turned, table[part, chunk, :, columns], preferred_element_type=jnp.float32
                 )
                 for part in range(2)
             )
@@ -355,7 +354,7 @@
     def out_copy(target, source):
         return pltpu.make_async_remote_copy(
             src_ref=signal_out.at[target],
-            dst_ref=signal_in.at[source],
+            dst_ref=out_ref.at[source],
             send_sem=out_send,
             recv_sem=out_recv,
             device_id=(det, target),
@@ -415,19 +414,8 @@
     for target in targets:
         send(target)
 
-    signal_in[me] = signal_out[me]
-    await_bytes(signal_in.at[pl.ds(0, count - 1)], out_recv)
-    wide[...] = signal_in[...].astype(jnp.float32).reshape(wide.shape)
-    rows_out = out_ref.shape[0]
-    for block in range(blocks):
-        parts = [
-            wide[pl.ds(first * blocks + block, 8, stride=blocks), :]
-            for first in range(0, rows_out, 8)
-        ]
-        out_ref[:, block * TILE : (block + 1) * TILE] = jnp.concatenate(parts, axis=0).astype(
-            out_ref.dtype
-        )
-
+    out_ref[me] = signal_out[me]
+    await_bytes(out_ref.at[pl.ds(0, count - 1)], out_recv)
     await_bytes(info.at[det, near, pl.ds(0, planes - 1)], info_send)
     await_bytes(info.at[det, pl.ds(0, PLANE - 1)], column_send)
     await_bytes(signal_out.at[pl.ds(0, count - 1)], out_send)
@@ -436,6 +424,15 @@
     for chunk in range(CHUNKS):
         pair_copy(chunk).wait_send()
     share_copy.wait_send()
+
+
+def lay_out(signal_ref, out_ref, wide):
+    rows, blocks = out_ref.shape[0], wide.shape[0] // out_ref.shape[0]
+    wide[...] = signal_ref[...].astype(jnp.float32).reshape(wide.shape)
+    for block in range(blocks):
+        out_ref[:, block * TILE : (block + 1) * TILE] = wide[
+            pl.ds(block, rows, stride=blocks), :
+        ]
 
 
 def local_fused(wigner, alm, beam, crossing, offsets, fraction, taps):
@@ -469,7 +466,7 @@
     arriving = pltpu.VMEM((count, CHUNKS, chunk_rows, items), bf16)
     result = pl.pallas_call(
         functools.partial(kernel, count, per, intervals, groups),
-        out_shape=jax.ShapeDtypeStruct((count * per, blocks * TILE), bf16),
+        out_shape=jax.ShapeDtypeStruct((count, per, blocks, TILE), bf16),
         in_specs=[
             anywhere, anywhere, anywhere, anywhere, vmem, vmem, vmem,
             pl.BlockSpec(memory_space=pltpu.SMEM),
@@ -494,8 +491,6 @@
             pltpu.VMEM((BATCH * TILE, per * TILE), f32),
             pltpu.VMEM((per, intervals * blocks + 16, TILE), f32),
             pltpu.VMEM((count, per, blocks, TILE), bf16),
-            pltpu.VMEM((count, per, blocks, TILE), bf16),
-            pltpu.VMEM((count * per * blocks, TILE), f32),
             dma((2,)), dma((CHUNKS,)), dma, dma, dma, dma, dma, dma, dma,
             dma((CHUNKS,)), dma((CHUNKS,)), dma((CHUNKS,)), dma((CHUNKS,)),
             dma, dma,
@@ -513,7 +508,14 @@
         fraction.reshape(blocks, TILE),
         taps,
     )
-    return result.astype(f32)
+    return pl.pallas_call(
+        lay_out,
+        grid=(count * per // 8,),
+        in_specs=[pl.BlockSpec((8 // per, per, blocks, TILE), lambda i: (i, 0, 0, 0))],
+        out_specs=pl.BlockSpec((8, blocks * TILE), lambda i: (i, 0)),
+        out_shape=jax.ShapeDtypeStruct((count * per, blocks * TILE), f32),
+        scratch_shapes=[pltpu.VMEM((8 * blocks, TILE), f32)],
+    )(result)
 
 
 def with_halo(cells, sides, width):

time: 38.2 us -> 39.7 us (1.039)
  Pallas kernels: 36.2 us -> 39.4 us
  other arithmetic: 1.78 us -> 0 us
    pallas_call x0 -> x1, Pallas kernels: none -> 3.18 us  [local_fused(): pl.pallas_call(lay_out, grid=(count * per // 8,), in_specs=[pl.BlockSpec(...]
    convert_element_type x1 -> x0, other arithmetic: 1.78 us -> none  [local_fused(): return result.astype(f32)]
where the time goes in v5:
time: 39.7 us; the launch traced here: 39.4 us
  Pallas kernels  39.4 us (99%)
    pallas_call x1, Pallas kernels, local_fused(): pl.pallas_call(functools.partial(kernel, count, per, intervals, groups),...  36.2 us
    pallas_call x1, Pallas kernels, local_fused(): pl.pallas_call(lay_out, grid=(count * per // 8,), in_specs=[pl.BlockSpec(...  3.18 us

profile of v5, /device:TPU:0, one launch (start us, length us, event | category | flops | bytes accessed | tf_op | source)
XLA Modules:
  0.0 39.4 jit_solution(2553688815771121354)
XLA Ops:
  0.0 36.2 %shard_map.82.signal_ref = bf16[16,2,32,128]{3,2,1,0:T(8,128)(2,1)} custom-call(bf16[16,2,128,1024]{3,2,1,0:T(8,128)(2,1)} %wigner_hbm.1, bf16[64,2,2048]{2,1,0:T(2,128)(2,1)} %beam_hbm.1, bf16[16,2,2048]{2,1,0:T(2,128)(2,1)} %alm_hbm.1, bf16[2,4,256,1024]{3,2,1,0:T(8,128)(2,1)} %constant.2.clone.table_hbm, s32[1,128]{1,0:T(1,128)} %crossing_ref.1, ...), custom_call_target="tpu_custom_call" | custom-call | tf_op jit(solution)/shard_map/pallas_call | solution.py:467
  36.2 3.2 %shard_map.83 = f32[32,4096]{1,0:T(8,128)} custom-call(bf16[16,2,32,128]{3,2,1,0:T(8,128)(2,1)} %shard_map.82.signal_ref), custom_call_target="tpu_custom_call" | custom-call | tf_op jit(solution)/shard_map/pallas_call | solution.py:511

commit v6 on v4

--- a/solution.py
+++ b/solution.py
@@ -10,7 +10,7 @@
 from jax.sharding import PartitionSpec as P
 
 TILE = 128
-CHUNKS = 4
+CHUNKS = 2
 PLANE = 4
 BATCH = 4
 INFO_ROWS = 40
@@ -164,9 +164,9 @@
     def multiply(chunk):
         wigner_copy(chunk).wait()
 
-        def pair(step, carry):
+        def pair(step):
             first = chunk * chunk_orders + 2 * step
-            place = pl.ds(pl.multiple_of(step * 2 * rows, 2 * rows), 2 * rows)
+            place = pl.ds(step * 2 * rows, 2 * rows)
             for beam_order in range(wigner.shape[1]):
                 lanes = pl.ds(beam_order * wigner.shape[2], wigner.shape[2])
                 one = product(first, beam_order)
@@ -179,9 +179,11 @@
                         ],
                         axis=1,
                     )
-            return carry
-
-        lax.fori_loop(0, chunk_orders // 2, pair, 0, unroll=True)
+
+        for step in range(chunk_orders // 2):
+            pair(step)
+            if step == chunk_orders // 4 - 1 and chunk > 0:
+                spread(chunk - 1)
 
     def pair_copy(chunk):
         return pltpu.make_async_remote_copy(
@@ -220,8 +222,6 @@
             for step in range(1, planes):
                 info_copy(step).start()
         pair_copy(chunk).start()
-        if chunk > 0:
-            spread(chunk - 1)
         if chunk == CHUNKS // 2:
             await_bytes(info.at[det, near, pl.ds(0, planes - 1)], info_recv)
             for step in range(1, PLANE):
@@ -268,13 +268,14 @@
     items = cube.shape[0] // groups
     half_rows = blocks // 2
 
+    places = lax.broadcasted_iota(jnp.int32, (TILE, TILE), 1).astype(jnp.float32)
+
     def prepare(n, carry):
         wanted = info[0, n % PLANE, n // PLANE, 2 * half_rows : 2 * half_rows + 1, :]
         ids = jnp.broadcast_to(wanted, (TILE, TILE)).T
         for part in range(cube.shape[0] // TILE):
-            places = lax.broadcasted_iota(jnp.int32, (TILE, TILE), 1) + part * TILE
             picks[n, :, part * TILE : (part + 1) * TILE] = jnp.where(
-                ids == places.astype(jnp.float32), 1.0, 0.0
+                ids - part * TILE == places, 1.0, 0.0
             ).astype(jnp.bfloat16)
         offset = jnp.concatenate([info[0, n % PLANE, n // PLANE, :half_rows], info[1, n % PLANE, n // PLANE, :half_rows]], axis=0)
         fraction = jnp.concatenate(
@@ -294,21 +295,19 @@
             )
         return carry
 
-    lax.fori_loop(0, intervals, prepare, 0)
+    lax.fori_loop(0, intervals, prepare, 0, unroll=2)
 
     table_copy.wait()
     chunk_rows = spectra_in.shape[2]
     for chunk in range(CHUNKS):
         await_bytes(spectra_in.at[pl.ds(0, count - 1), chunk], spec_recv.at[chunk])
         spectra = spectra_in[:, chunk].reshape(count * chunk_rows, items)
+        turned = spectra.T
         for b in range(groups):
             columns = pl.ds(b * per * TILE, per * TILE)
             total = sum(
-                lax.dot_general(
-                    spectra,
-                    table[part, chunk, :, columns],
-                    (((0,), (0,)), ((), ())),
-                    preferred_element_type=jnp.float32,
+                jnp.dot(
+                    turned, table[part, chunk, :, columns], preferred_element_type=jnp.float32
                 )
                 for part in range(2)
             )
@@ -691,7 +690,7 @@
     return (
         mesh.shape["det"] == 2
         and beam.shape[0] == 4 * count
-        and wigner.shape[0] == 4 * CHUNKS * count
+        and wigner.shape[0] == 16 * count
         and 2 * wigner.shape[0] == 4 * TILE
         and wigner.shape[1:3] == (2, TILE)
         and offsets.shape == (count, 32 * TILE)

time: 38.2 us -> 39.3 us (1.029)
  Pallas kernels: 36.2 us -> 37.3 us
    pallas_call x1, Pallas kernels: 36.2 us -> 37.3 us  [local_fused(): pl.pallas_call(functools.partial(kernel, count, per, intervals, groups),...]
where the time goes in v6:
time: 39.3 us; the launch traced here: 39.1 us
  Pallas kernels  37.3 us (95%)
  other arithmetic  1.78 us (5%)
    pallas_call x1, Pallas kernels, local_fused(): pl.pallas_call(functools.partial(kernel, count, per, intervals, groups),...  37.3 us
    convert_element_type x1, other arithmetic, local_fused(): return result.astype(f32)  1.78 us

profile of v6, /device:TPU:0, one launch (start us, length us, event | category | flops | bytes accessed | tf_op | source)
XLA Modules:
  0.0 39.1 jit_solution(11489353308089110889)
XLA Ops:
  0.0 37.3 %shard_map.82 = bf16[32,4096]{1,0:T(8,128)(2,1)} custom-call(bf16[16,2,128,1024]{3,2,1,0:T(8,128)(2,1)} %wigner_hbm.1, bf16[64,2,2048]{2,1,0:T(2,128)(2,1)} %beam_hbm.1, bf16[16,2,2048]{2,1,0:T(2,128)(2,1)} %alm_hbm.1, bf16[2,2,512,1024]{3,2,1,0:T(8,128)(2,1)} %constant.2.clone.table_hbm, s32[1,128]{1,0:T(1,128)} %crossing_ref.1, s32[32,128]{1,0:T(8,128)} %bitcast.2, ...), custom_call_target="tpu_custom_call" | custom-call | tf_op jit(solution)/shard_map/pallas_call | solution.py:469
  37.3 1.8 %convert_element_type.3 = f32[32,4096]{1,0:T(8,128)} convert(bf16[32,4096]{1,0:T(8,128)(2,1)} %shard_map.82) | non-fusion elementwise | flops 131072 | bytes 786432 | tf_op jit(solution)/shard_map/convert_element_type | solution.py:515
